TPU v7x, 32 devices: a whole 2x2x4 slice. The times are simulated.
32 devices in a mesh: section: 2 (over core), dp: 16 (over z, y, x).
Axes of the slice: x: 2, y: 2, z: 4, core: 2. Of those that a mesh axis runs over, the one named last changes fastest.
Arguments:
- inputs: bfloat16 [8, 16, 32, 64, 128], P(None, 'dp'), may hold values from -66 to 66
- channel_mean: float32 [128], replicated, may hold values from -3 to 3
- channel_std: float32 [128], replicated, may hold values from 0.5 to 2
- cotangent: bfloat16 [8, 16, 32, 64, 128], P(None, 'dp'), may hold values from -15 to 15
- conv_w1: bfloat16 [2, 3, 3, 128, 128], P('section'), may hold values from -0.1875 to 0.1875
- conv_b1: float32 [2, 128], P('section'), may hold values from -3 to 3
- bn_gain1: float32 [2, 128], P('section'), may hold values from 0.25 to 1.75
- bn_shift1: float32 [2, 128], P('section'), may hold values from -3 to 3
- conv_w2: bfloat16 [2, 3, 3, 128, 128], P('section'), may hold values from -0.1875 to 0.1875
- conv_b2: float32 [2, 128], P('section'), may hold values from -3 to 3
- bn_gain2: float32 [2, 128], P('section'), may hold values from 0.25 to 1.75
- bn_shift2: float32 [2, 128], P('section'), may hold values from -3 to 3
Outputs:
- block_outputs: bfloat16 [2, 8, 16, 32, 64, 128], P('section', None, 'dp')
- edge_grads: bfloat16 [2, 8, 16, 32, 64, 128], P('section', None, 'dp')
- grad_w1: float32 [2, 3, 3, 128, 128], P('section')
- grad_b1: float32 [2, 128], P('section')
- grad_gain1: float32 [2, 128], P('section')
- grad_shift1: float32 [2, 128], P('section')
- grad_w2: float32 [2, 3, 3, 128, 128], P('section')
- grad_b2: float32 [2, 128], P('section')
- grad_gain2: float32 [2, 128], P('section')
- grad_shift2: float32 [2, 128], P('section')
All inputs are finite; a program needn't handle non-finite values.
Results may differ from a plain program's by a relative error of at most 0.011.
Values may be sent and summed in bfloat16 or wider, within the bound.
A program may use at most 128 MiB of HBM per device.

v0:
```python
import jax
import jax.numpy as jnp
from jax import lax
from jax.sharding import PartitionSpec as P

norm_eps = 1e-05


def passed_along(block, axis, distance):
    devices = range(lax.axis_size(axis))
    route = [(i - distance, i) for i in devices if i - distance in devices]
    return lax.ppermute(block, axis, route)


def pad_grid(field_in):
    wrapped = jnp.concatenate([field_in[:, :, -1:], field_in, field_in[:, :, :1]], axis=2)
    return jnp.pad(wrapped, ((0, 0), (1, 1), (0, 0), (0, 0)))


def conv_apply(field_in, kernel):
    return lax.conv_general_dilated(
        pad_grid(field_in),
        kernel,
        (1, 1),
        "VALID",
        dimension_numbers=("NHWC", "HWIO", "NHWC"),
        preferred_element_type=jnp.float32,
    )


def conv_back(grad_low, kernel):
    flipped = jnp.transpose(kernel[::-1, ::-1], (0, 1, 3, 2))
    return conv_apply(grad_low, flipped)


def kernel_grad(field_in, grad_low):
    padded = pad_grid(field_in)
    height = grad_low.shape[1]
    extent = grad_low.shape[2]
    all_taps = []
    for tap_row in range(3):
        row_taps = []
        for tap_col in range(3):
            window = padded[:, tap_row : tap_row + height, tap_col : tap_col + extent]
            row_taps.append(
                jnp.einsum("nhwc,nhwd->cd", window, grad_low, preferred_element_type=jnp.float32)
            )
        all_taps.append(jnp.stack(row_taps))
    return jnp.stack(all_taps)


def silu_slope(pre_act):
    sigmoid = jax.nn.sigmoid(pre_act)
    return sigmoid * (1.0 + pre_act * (1.0 - sigmoid))


def moments(activ, pixel_count):
    totals, squares = lax.psum(
        (jnp.sum(activ, axis=(0, 1, 2)), jnp.sum(activ * activ, axis=(0, 1, 2))), "dp"
    )
    center = totals / pixel_count
    spread = lax.rsqrt(squares / pixel_count - center * center + norm_eps)
    return (center, spread)


def forward_block(skip_in, params, pixel_count):
    w_one, b_one, g_one, s_one, w_two, b_two, g_two, s_two = params
    conv_in = skip_in.astype(jnp.bfloat16)
    pre_one = conv_apply(conv_in, w_one) + b_one
    act_one = jax.nn.silu(pre_one)
    center_one, spread_one = moments(act_one, pixel_count)
    normed_one = ((act_one - center_one) * spread_one * g_one + s_one).astype(jnp.bfloat16)
    pre_two = conv_apply(normed_one, w_two) + b_two
    act_two = jax.nn.silu(pre_two)
    center_two, spread_two = moments(act_two, pixel_count)
    block_out = skip_in + ((act_two - center_two) * spread_two * g_two + s_two)
    stat_rows = jnp.stack([center_one, spread_one, center_two, spread_two])
    return (block_out, conv_in, pre_one, normed_one, pre_two, stat_rows)


def norm_back(grad_norm, pre_act, center, spread, gain, pixel_count):
    normal_form = (jax.nn.silu(pre_act) - center) * spread
    shift_sum, gain_sum = lax.psum(
        (jnp.sum(grad_norm, axis=(0, 1, 2)), jnp.sum(grad_norm * normal_form, axis=(0, 1, 2))), "dp"
    )
    grad_act = (
        gain * spread * (grad_norm - shift_sum / pixel_count - normal_form * gain_sum / pixel_count)
    )
    return (grad_act * silu_slope(pre_act), shift_sum, gain_sum)


def backward_block(grad_out, conv_in, pre_one, normed_one, pre_two, stat_rows, params, pixel_count):
    w_one, b_one, g_one, s_one, w_two, b_two, g_two, s_two = params
    grad_pre_two, shift_two, gain_two = norm_back(
        grad_out, pre_two, stat_rows[2], stat_rows[3], g_two, pixel_count
    )
    low_two = grad_pre_two.astype(jnp.bfloat16)
    kernel_two = kernel_grad(normed_one, low_two)
    grad_normed = conv_back(low_two, w_two)
    grad_pre_one, shift_one, gain_one = norm_back(
        grad_normed, pre_one, stat_rows[0], stat_rows[1], g_one, pixel_count
    )
    low_one = grad_pre_one.astype(jnp.bfloat16)
    kernel_one = kernel_grad(conv_in, low_one)
    grad_in = grad_out + conv_back(low_one, w_one)
    local_parts = (
        kernel_one,
        jnp.sum(grad_pre_one, axis=(0, 1, 2)),
        kernel_two,
        jnp.sum(grad_pre_two, axis=(0, 1, 2)),
    )
    norm_parts = (gain_one, shift_one, gain_two, shift_two)
    return (grad_in, local_parts, norm_parts)


def put_slot(holder, new_item, slot_pos, usable):
    previous = lax.dynamic_index_in_dim(holder, slot_pos, 0, keepdims=False)
    return lax.dynamic_update_index_in_dim(
        holder, jnp.where(usable, new_item, previous), slot_pos, 0
    )


def per_device(
    inputs,
    channel_mean,
    channel_std,
    cotangent,
    conv_w1,
    conv_b1,
    bn_gain1,
    bn_shift1,
    conv_w2,
    conv_b2,
    bn_gain2,
    bn_shift2,
):
    params = (
        conv_w1[0],
        conv_b1[0],
        bn_gain1[0],
        bn_shift1[0],
        conv_w2[0],
        conv_b2[0],
        bn_gain2[0],
        bn_shift2[0],
    )
    micro_count = inputs.shape[0]
    local_shape = inputs.shape[1:]
    channels = local_shape[3]
    pixel_count = float(local_shape[0] * local_shape[1] * local_shape[2] * lax.axis_size("dp"))
    section_pos = lax.axis_index("section")
    is_first = section_pos == 0
    low_zero = jnp.zeros((micro_count,) + local_shape, jnp.bfloat16)
    high_zero = jnp.zeros((micro_count,) + local_shape, jnp.float32)
    stat_zero = jnp.zeros((micro_count, 4, channels), jnp.float32)
    kept_sets = (low_zero, high_zero, low_zero, high_zero, stat_zero)

    def forward_tick(tick_pos, carry_in):
        incoming, outputs_kept, kept_now = carry_in
        batch_pos = tick_pos - section_pos
        slot_pos = jnp.clip(batch_pos, 0, micro_count - 1)
        usable = (batch_pos >= 0) & (batch_pos < micro_count)
        raw_in = lax.dynamic_index_in_dim(inputs, slot_pos, 0, keepdims=False).astype(jnp.float32)
        scaled = (raw_in - channel_mean) / channel_std
        skip_in = jnp.where(is_first, scaled, incoming.astype(jnp.float32))
        block_out, conv_in, pre_one, normed_one, pre_two, stat_rows = forward_block(
            skip_in, params, pixel_count
        )
        out_low = block_out.astype(jnp.bfloat16)
        outputs_kept = put_slot(outputs_kept, out_low, slot_pos, usable)
        fresh = (conv_in, pre_one, normed_one, pre_two, stat_rows)
        kept_now = tuple(
            (
                put_slot(holder, new_item, slot_pos, usable)
                for holder, new_item in zip(kept_now, fresh)
            )
        )
        incoming = passed_along(out_low, "section", 1)
        return (incoming, outputs_kept, kept_now)

    start_act = jnp.zeros(local_shape, jnp.bfloat16)
    unused_act, outputs_kept, kept_sets = lax.fori_loop(
        0, micro_count + 1, forward_tick, (start_act, low_zero, kept_sets)
    )
    kernel_zero = jnp.zeros(conv_w1.shape[1:], jnp.float32)
    chan_zero = jnp.zeros((channels,), jnp.float32)
    local_start = (kernel_zero, chan_zero, kernel_zero, chan_zero)
    norm_start = (chan_zero, chan_zero, chan_zero, chan_zero)

    def backward_tick(tick_pos, carry_in):
        returned, grads_kept, local_sum, norm_sum = carry_in
        batch_pos = tick_pos - 1 + section_pos
        slot_pos = jnp.clip(batch_pos, 0, micro_count - 1)
        usable = (batch_pos >= 0) & (batch_pos < micro_count)
        given_grad = lax.dynamic_index_in_dim(cotangent, slot_pos, 0, keepdims=False).astype(
            jnp.float32
        )
        given_grad = given_grad * usable.astype(jnp.float32)
        grad_out = jnp.where(is_first, returned.astype(jnp.float32), given_grad)
        entry_set = tuple(
            (lax.dynamic_index_in_dim(holder, slot_pos, 0, keepdims=False) for holder in kept_sets)
        )
        conv_in, pre_one, normed_one, pre_two, stat_rows = entry_set
        grad_in, local_parts, norm_parts = backward_block(
            grad_out, conv_in, pre_one, normed_one, pre_two, stat_rows, params, pixel_count
        )
        edge_grad = jnp.where(is_first, grad_in / channel_std, grad_in).astype(jnp.bfloat16)
        grads_kept = put_slot(grads_kept, edge_grad, slot_pos, usable)
        summed = lax.psum((local_parts[0], local_parts[1], local_parts[2], local_parts[3]), "dp")
        local_sum = tuple(
            (total_part + new_part for total_part, new_part in zip(local_sum, summed))
        )
        norm_sum = tuple(
            (total_part + new_part for total_part, new_part in zip(norm_sum, norm_parts))
        )
        returned = passed_along(grad_in.astype(jnp.bfloat16), "section", -1)
        return (returned, grads_kept, local_sum, norm_sum)

    start_grad = jnp.zeros(local_shape, jnp.bfloat16)
    unused_grad, grads_kept, local_sum, norm_sum = lax.fori_loop(
        0, micro_count + 1, backward_tick, (start_grad, low_zero, local_start, norm_start)
    )
    return (
        outputs_kept[None],
        grads_kept[None],
        local_sum[0][None],
        local_sum[1][None],
        norm_sum[0][None],
        norm_sum[1][None],
        local_sum[2][None],
        local_sum[3][None],
        norm_sum[2][None],
        norm_sum[3][None],
    )


def solution(mesh):
    in_specs = (
        P(None, "dp", None, None, None),
        P(),
        P(),
        P(None, "dp", None, None, None),
        P("section", None, None, None, None),
        P("section", None),
        P("section", None),
        P("section", None),
        P("section", None, None, None, None),
        P("section", None),
        P("section", None),
        P("section", None),
    )
    out_specs = (
        P("section", None, "dp", None, None, None),
        P("section", None, "dp", None, None, None),
        P("section", None, None, None, None),
        P("section", None),
        P("section", None),
        P("section", None),
        P("section", None, None, None, None),
        P("section", None),
        P("section", None),
        P("section", None),
    )
    return jax.shard_map(
        per_device, mesh=mesh, in_specs=in_specs, out_specs=out_specs, check_vma=False
    )
```

profile of v0, /device:TPU:0, one launch (start us, length us, event | category | flops | bytes accessed | tf_op | source)
XLA Modules:
  0.0 2971.2 jit_solution(15090785682176913330)
XLA Ops:
  25.2 941.4 %while.61 = (s32[]{:T(128)}, bf16[1,32,64,128]{3,1,2,0:T(8,128)(2,1)}, bf16[8,1,32,64,128]{4,3,2,0,1:T(8,128)(2,1)}, bf16[8,1,32,64,128]{4,2,3,1,0:T(8,128)(2,1)...) while((s32[]{:T(128)}, ...), condition=%wide.region_9.10_spmd, body=%wide.region_0.9_spmd.sunk | while | flops 1352273152 | bytes 58811492 | solution.py:182
  33.1 43.5 %all-reduce.14 = (f32[128]{0:T(128)S(1)}, f32[128]{0:T(128)S(1)}) all-reduce(f32[128]{0:T(128)S(1)} %get-tuple-element.1666, f32[128]{0:T(128)S(1)} %get-tuple-element.1667), channel_id=1, replica_groups=mesh['section'=2,'dp'=16] {'dp'}, use_global_device_ids=true, to_apply=%region_4.4 | all-reduce | flops 256 | bytes 2048 | tf_op jit(solution)/shard_map/while/body/eval_jaxpr/psum | solution.py:58
  969.8 1994.0 %while.62 = (s32[]{:T(128)}, bf16[1,32,64,128]{3,1,2,0:T(8,128)(2,1)S(1)}, bf16[8,1,32,64,128]{4,3,2,0,1:T(8,128)(2,1)}, f32[3,3,128,128]{3,2,1,0:T(8,128)S(1)},...) while((s32[]{:T(128)}, ...), condition=%wide.region_25.26_spmd.clone, body=%wide.region_10.25_spmd.clone.sunk | while | flops 2578298880 | bytes 91627768 | solution.py:220
  1118.2 70.1 %all-reduce.22.cloned.1.call-done = (f32[3,3,128,128]{3,2,1,0:T(8,128)}, f32[3,3,128,128]{3,2,1,0:T(8,128)}) async-done(((f32[3,3,128,128]{3,2,1,0:T(8,128)}, f32[3,3,128,128]{3,2,1,0:T(8,128)}), (f32[3,3,128,128]{3,2,1,0:T(8,128)}, f32[3,3,128,128]{3,2,1,0:T(8,128)})) %all-reduce.22.cloned.1.call-update) | async-done | bytes 1179664 | tf_op jit(solution)/shard_map/while/body/eval_jaxpr/psum | solution.py:209
  1193.7 39.7 %all-reduce.16 = (f32[128]{0:T(128)S(1)}, f32[128]{0:T(128)S(1)}) all-reduce(f32[128]{0:T(128)S(1)} %get-tuple-element.1715, f32[128]{0:T(128)S(1)} %get-tuple-element.1716), channel_id=1, replica_groups=mesh['section'=2,'dp'=16] {'dp'}, use_global_device_ids=true, to_apply=%region_14.14 | all-reduce | flops 256 | bytes 2048 | tf_op jit(solution)/shard_map/while/body/eval_jaxpr/psum | solution.py:83
  1339.9 70.1 %all-reduce.22.cloned.1.call-done = (f32[3,3,128,128]{3,2,1,0:T(8,128)}, f32[3,3,128,128]{3,2,1,0:T(8,128)}) async-done(((f32[3,3,128,128]{3,2,1,0:T(8,128)}, f32[3,3,128,128]{3,2,1,0:T(8,128)}), (f32[3,3,128,128]{3,2,1,0:T(8,128)}, f32[3,3,128,128]{3,2,1,0:T(8,128)})) %all-reduce.22.cloned.1.call-update) | async-done | bytes 1179664 | tf_op jit(solution)/shard_map/while/body/eval_jaxpr/psum | solution.py:209
  1415.4 39.7 %all-reduce.16 = (f32[128]{0:T(128)S(1)}, f32[128]{0:T(128)S(1)}) all-reduce(f32[128]{0:T(128)S(1)} %get-tuple-element.1715, f32[128]{0:T(128)S(1)} %get-tuple-element.1716), channel_id=1, replica_groups=mesh['section'=2,'dp'=16] {'dp'}, use_global_device_ids=true, to_apply=%region_14.14 | all-reduce | flops 256 | bytes 2048 | tf_op jit(solution)/shard_map/while/body/eval_jaxpr/psum | solution.py:83
  1520.4 39.1 %all-reduce.19 = (f32[128]{0:T(128)S(1)}, f32[128]{0:T(128)S(1)}) all-reduce(f32[128]{0:T(128)S(1)} %get-tuple-element.1742, f32[128]{0:T(128)S(1)} %get-tuple-element.1743), channel_id=1, replica_groups=mesh['section'=2,'dp'=16] {'dp'}, use_global_device_ids=true, to_apply=%region_21.21 | all-reduce | flops 256 | bytes 2048 | tf_op jit(solution)/shard_map/while/body/eval_jaxpr/psum | solution.py:209
  1561.6 69.9 %all-reduce.22.cloned.1.call-done = (f32[3,3,128,128]{3,2,1,0:T(8,128)}, f32[3,3,128,128]{3,2,1,0:T(8,128)}) async-done(((f32[3,3,128,128]{3,2,1,0:T(8,128)}, f32[3,3,128,128]{3,2,1,0:T(8,128)}), (f32[3,3,128,128]{3,2,1,0:T(8,128)}, f32[3,3,128,128]{3,2,1,0:T(8,128)})) %all-reduce.22.cloned.1.call-update) | async-done | bytes 1179664 | tf_op jit(solution)/shard_map/while/body/eval_jaxpr/psum | solution.py:209
  1637.0 39.7 %all-reduce.16 = (f32[128]{0:T(128)S(1)}, f32[128]{0:T(128)S(1)}) all-reduce(f32[128]{0:T(128)S(1)} %get-tuple-element.1715, f32[128]{0:T(128)S(1)} %get-tuple-element.1716), channel_id=1, replica_groups=mesh['section'=2,'dp'=16] {'dp'}, use_global_device_ids=true, to_apply=%region_14.14 | all-reduce | flops 256 | bytes 2048 | tf_op jit(solution)/shard_map/while/body/eval_jaxpr/psum | solution.py:83
  1783.2 70.0 %all-reduce.22.cloned.1.call-done = (f32[3,3,128,128]{3,2,1,0:T(8,128)}, f32[3,3,128,128]{3,2,1,0:T(8,128)}) async-done(((f32[3,3,128,128]{3,2,1,0:T(8,128)}, f32[3,3,128,128]{3,2,1,0:T(8,128)}), (f32[3,3,128,128]{3,2,1,0:T(8,128)}, f32[3,3,128,128]{3,2,1,0:T(8,128)})) %all-reduce.22.cloned.1.call-update) | async-done | bytes 1179664 | tf_op jit(solution)/shard_map/while/body/eval_jaxpr/psum | solution.py:209
  1858.6 39.7 %all-reduce.16 = (f32[128]{0:T(128)S(1)}, f32[128]{0:T(128)S(1)}) all-reduce(f32[128]{0:T(128)S(1)} %get-tuple-element.1715, f32[128]{0:T(128)S(1)} %get-tuple-element.1716), channel_id=1, replica_groups=mesh['section'=2,'dp'=16] {'dp'}, use_global_device_ids=true, to_apply=%region_14.14 | all-reduce | flops 256 | bytes 2048 | tf_op jit(solution)/shard_map/while/body/eval_jaxpr/psum | solution.py:83
  1963.7 39.1 %all-reduce.19 = (f32[128]{0:T(128)S(1)}, f32[128]{0:T(128)S(1)}) all-reduce(f32[128]{0:T(128)S(1)} %get-tuple-element.1742, f32[128]{0:T(128)S(1)} %get-tuple-element.1743), channel_id=1, replica_groups=mesh['section'=2,'dp'=16] {'dp'}, use_global_device_ids=true, to_apply=%region_21.21 | all-reduce | flops 256 | bytes 2048 | tf_op jit(solution)/shard_map/while/body/eval_jaxpr/psum | solution.py:209
  2004.9 69.9 %all-reduce.22.cloned.1.call-done = (f32[3,3,128,128]{3,2,1,0:T(8,128)}, f32[3,3,128,128]{3,2,1,0:T(8,128)}) async-done(((f32[3,3,128,128]{3,2,1,0:T(8,128)}, f32[3,3,128,128]{3,2,1,0:T(8,128)}), (f32[3,3,128,128]{3,2,1,0:T(8,128)}, f32[3,3,128,128]{3,2,1,0:T(8,128)})) %all-reduce.22.cloned.1.call-update) | async-done | bytes 1179664 | tf_op jit(solution)/shard_map/while/body/eval_jaxpr/psum | solution.py:209
  2080.2 39.7 %all-reduce.16 = (f32[128]{0:T(128)S(1)}, f32[128]{0:T(128)S(1)}) all-reduce(f32[128]{0:T(128)S(1)} %get-tuple-element.1715, f32[128]{0:T(128)S(1)} %get-tuple-element.1716), channel_id=1, replica_groups=mesh['section'=2,'dp'=16] {'dp'}, use_global_device_ids=true, to_apply=%region_14.14 | all-reduce | flops 256 | bytes 2048 | tf_op jit(solution)/shard_map/while/body/eval_jaxpr/psum | solution.py:83
  2226.4 70.0 %all-reduce.22.cloned.1.call-done = (f32[3,3,128,128]{3,2,1,0:T(8,128)}, f32[3,3,128,128]{3,2,1,0:T(8,128)}) async-done(((f32[3,3,128,128]{3,2,1,0:T(8,128)}, f32[3,3,128,128]{3,2,1,0:T(8,128)}), (f32[3,3,128,128]{3,2,1,0:T(8,128)}, f32[3,3,128,128]{3,2,1,0:T(8,128)})) %all-reduce.22.cloned.1.call-update) | async-done | bytes 1179664 | tf_op jit(solution)/shard_map/while/body/eval_jaxpr/psum | solution.py:209
  2301.9 39.7 %all-reduce.16 = (f32[128]{0:T(128)S(1)}, f32[128]{0:T(128)S(1)}) all-reduce(f32[128]{0:T(128)S(1)} %get-tuple-element.1715, f32[128]{0:T(128)S(1)} %get-tuple-element.1716), channel_id=1, replica_groups=mesh['section'=2,'dp'=16] {'dp'}, use_global_device_ids=true, to_apply=%region_14.14 | all-reduce | flops 256 | bytes 2048 | tf_op jit(solution)/shard_map/while/body/eval_jaxpr/psum | solution.py:83
  2407.0 39.1 %all-reduce.19 = (f32[128]{0:T(128)S(1)}, f32[128]{0:T(128)S(1)}) all-reduce(f32[128]{0:T(128)S(1)} %get-tuple-element.1742, f32[128]{0:T(128)S(1)} %get-tuple-element.1743), channel_id=1, replica_groups=mesh['section'=2,'dp'=16] {'dp'}, use_global_device_ids=true, to_apply=%region_21.21 | all-reduce | flops 256 | bytes 2048 | tf_op jit(solution)/shard_map/while/body/eval_jaxpr/psum | solution.py:209
  2448.1 69.9 %all-reduce.22.cloned.1.call-done = (f32[3,3,128,128]{3,2,1,0:T(8,128)}, f32[3,3,128,128]{3,2,1,0:T(8,128)}) async-done(((f32[3,3,128,128]{3,2,1,0:T(8,128)}, f32[3,3,128,128]{3,2,1,0:T(8,128)}), (f32[3,3,128,128]{3,2,1,0:T(8,128)}, f32[3,3,128,128]{3,2,1,0:T(8,128)})) %all-reduce.22.cloned.1.call-update) | async-done | bytes 1179664 | tf_op jit(solution)/shard_map/while/body/eval_jaxpr/psum | solution.py:209
  2523.5 39.7 %all-reduce.16 = (f32[128]{0:T(128)S(1)}, f32[128]{0:T(128)S(1)}) all-reduce(f32[128]{0:T(128)S(1)} %get-tuple-element.1715, f32[128]{0:T(128)S(1)} %get-tuple-element.1716), channel_id=1, replica_groups=mesh['section'=2,'dp'=16] {'dp'}, use_global_device_ids=true, to_apply=%region_14.14 | all-reduce | flops 256 | bytes 2048 | tf_op jit(solution)/shard_map/while/body/eval_jaxpr/psum | solution.py:83
  2669.7 70.0 %all-reduce.22.cloned.1.call-done = (f32[3,3,128,128]{3,2,1,0:T(8,128)}, f32[3,3,128,128]{3,2,1,0:T(8,128)}) async-done(((f32[3,3,128,128]{3,2,1,0:T(8,128)}, f32[3,3,128,128]{3,2,1,0:T(8,128)}), (f32[3,3,128,128]{3,2,1,0:T(8,128)}, f32[3,3,128,128]{3,2,1,0:T(8,128)})) %all-reduce.22.cloned.1.call-update) | async-done | bytes 1179664 | tf_op jit(solution)/shard_map/while/body/eval_jaxpr/psum | solution.py:209
  2745.2 39.7 %all-reduce.16 = (f32[128]{0:T(128)S(1)}, f32[128]{0:T(128)S(1)}) all-reduce(f32[128]{0:T(128)S(1)} %get-tuple-element.1715, f32[128]{0:T(128)S(1)} %get-tuple-element.1716), channel_id=1, replica_groups=mesh['section'=2,'dp'=16] {'dp'}, use_global_device_ids=true, to_apply=%region_14.14 | all-reduce | flops 256 | bytes 2048 | tf_op jit(solution)/shard_map/while/body/eval_jaxpr/psum | solution.py:83
  2850.2 39.1 %all-reduce.19 = (f32[128]{0:T(128)S(1)}, f32[128]{0:T(128)S(1)}) all-reduce(f32[128]{0:T(128)S(1)} %get-tuple-element.1742, f32[128]{0:T(128)S(1)} %get-tuple-element.1743), channel_id=1, replica_groups=mesh['section'=2,'dp'=16] {'dp'}, use_global_device_ids=true, to_apply=%region_21.21 | all-reduce | flops 256 | bytes 2048 | tf_op jit(solution)/shard_map/while/body/eval_jaxpr/psum | solution.py:209
  2891.4 69.9 %all-reduce.22.cloned.1.call-done = (f32[3,3,128,128]{3,2,1,0:T(8,128)}, f32[3,3,128,128]{3,2,1,0:T(8,128)}) async-done(((f32[3,3,128,128]{3,2,1,0:T(8,128)}, f32[3,3,128,128]{3,2,1,0:T(8,128)}), (f32[3,3,128,128]{3,2,1,0:T(8,128)}, f32[3,3,128,128]{3,2,1,0:T(8,128)})) %all-reduce.22.cloned.1.call-update) | async-done | bytes 1179664 | tf_op jit(solution)/shard_map/while/body/eval_jaxpr/psum | solution.py:209
  (1179 shorter events, 1805.2 us)
Async XLA Ops:
  121.2 13.2 collective-permute-start
  329.2 13.2 collective-permute-start
  433.3 13.2 collective-permute-start
  537.3 13.2 collective-permute-start
  849.3 13.3 collective-permute-start
  953.4 13.3 collective-permute-start
  970.1 218.2 %all-reduce.22.cloned.1.call-start = ((), (), s32[]{:S(2)}) async-start(), calls=%async_computation | async-start | bytes 2359296 | tf_op jit(solution)/shard_map/while/body/eval_jaxpr/psum | solution.py:209
  1061.2 56.0 %collective-permute-start.1 = (bf16[1,32,64,128]{3,1,2,0:T(8,128)(2,1)}, bf16[1,32,64,128]{3,1,2,0:T(8,128)(2,1)}, u32[]{:S(2)}, u32[]{:S(2)}) collective-permute-start(bf16[1,32,64,128]{3,1,2,0:T(8,128)(2,1)} %fusion.249), channel_id=1, source_target_pairs={{16,0},{17,1},{18,2},{19,3},{20,4},{21,5},{22,6},{23,7},{24,8},{25... | collective-permute-start | bytes 1572872 | tf_op jit(solution)/shard_map/while/body/eval_jaxpr/ppermute | solution.py:12
  1190.7 219.2 %all-reduce.22.cloned.1.call-start = ((), (), s32[]{:S(2)}) async-start(), calls=%async_computation | async-start | bytes 2359296 | tf_op jit(solution)/shard_map/while/body/eval_jaxpr/psum | solution.py:209
  1282.8 56.0 %collective-permute-start.1 = (bf16[1,32,64,128]{3,1,2,0:T(8,128)(2,1)}, bf16[1,32,64,128]{3,1,2,0:T(8,128)(2,1)}, u32[]{:S(2)}, u32[]{:S(2)}) collective-permute-start(bf16[1,32,64,128]{3,1,2,0:T(8,128)(2,1)} %fusion.249), channel_id=1, source_target_pairs={{16,0},{17,1},{18,2},{19,3},{20,4},{21,5},{22,6},{23,7},{24,8},{25... | collective-permute-start | bytes 1572872 | tf_op jit(solution)/shard_map/while/body/eval_jaxpr/ppermute | solution.py:12
  1412.4 219.1 %all-reduce.22.cloned.1.call-start = ((), (), s32[]{:S(2)}) async-start(), calls=%async_computation | async-start | bytes 2359296 | tf_op jit(solution)/shard_map/while/body/eval_jaxpr/psum | solution.py:209
  1504.5 56.0 %collective-permute-start.1 = (bf16[1,32,64,128]{3,1,2,0:T(8,128)(2,1)}, bf16[1,32,64,128]{3,1,2,0:T(8,128)(2,1)}, u32[]{:S(2)}, u32[]{:S(2)}) collective-permute-start(bf16[1,32,64,128]{3,1,2,0:T(8,128)(2,1)} %fusion.249), channel_id=1, source_target_pairs={{16,0},{17,1},{18,2},{19,3},{20,4},{21,5},{22,6},{23,7},{24,8},{25... | collective-permute-start | bytes 1572872 | tf_op jit(solution)/shard_map/while/body/eval_jaxpr/ppermute | solution.py:12
  1634.0 219.2 %all-reduce.22.cloned.1.call-start = ((), (), s32[]{:S(2)}) async-start(), calls=%async_computation | async-start | bytes 2359296 | tf_op jit(solution)/shard_map/while/body/eval_jaxpr/psum | solution.py:209
  1726.1 56.0 %collective-permute-start.1 = (bf16[1,32,64,128]{3,1,2,0:T(8,128)(2,1)}, bf16[1,32,64,128]{3,1,2,0:T(8,128)(2,1)}, u32[]{:S(2)}, u32[]{:S(2)}) collective-permute-start(bf16[1,32,64,128]{3,1,2,0:T(8,128)(2,1)} %fusion.249), channel_id=1, source_target_pairs={{16,0},{17,1},{18,2},{19,3},{20,4},{21,5},{22,6},{23,7},{24,8},{25... | collective-permute-start | bytes 1572872 | tf_op jit(solution)/shard_map/while/body/eval_jaxpr/ppermute | solution.py:12
  1855.7 219.1 %all-reduce.22.cloned.1.call-start = ((), (), s32[]{:S(2)}) async-start(), calls=%async_computation | async-start | bytes 2359296 | tf_op jit(solution)/shard_map/while/body/eval_jaxpr/psum | solution.py:209
  1947.8 56.0 %collective-permute-start.1 = (bf16[1,32,64,128]{3,1,2,0:T(8,128)(2,1)}, bf16[1,32,64,128]{3,1,2,0:T(8,128)(2,1)}, u32[]{:S(2)}, u32[]{:S(2)}) collective-permute-start(bf16[1,32,64,128]{3,1,2,0:T(8,128)(2,1)} %fusion.249), channel_id=1, source_target_pairs={{16,0},{17,1},{18,2},{19,3},{20,4},{21,5},{22,6},{23,7},{24,8},{25... | collective-permute-start | bytes 1572872 | tf_op jit(solution)/shard_map/while/body/eval_jaxpr/ppermute | solution.py:12
  2077.3 219.2 %all-reduce.22.cloned.1.call-start = ((), (), s32[]{:S(2)}) async-start(), calls=%async_computation | async-start | bytes 2359296 | tf_op jit(solution)/shard_map/while/body/eval_jaxpr/psum | solution.py:209
  2169.4 56.0 %collective-permute-start.1 = (bf16[1,32,64,128]{3,1,2,0:T(8,128)(2,1)}, bf16[1,32,64,128]{3,1,2,0:T(8,128)(2,1)}, u32[]{:S(2)}, u32[]{:S(2)}) collective-permute-start(bf16[1,32,64,128]{3,1,2,0:T(8,128)(2,1)} %fusion.249), channel_id=1, source_target_pairs={{16,0},{17,1},{18,2},{19,3},{20,4},{21,5},{22,6},{23,7},{24,8},{25... | collective-permute-start | bytes 1572872 | tf_op jit(solution)/shard_map/while/body/eval_jaxpr/ppermute | solution.py:12
  2299.0 219.1 %all-reduce.22.cloned.1.call-start = ((), (), s32[]{:S(2)}) async-start(), calls=%async_computation | async-start | bytes 2359296 | tf_op jit(solution)/shard_map/while/body/eval_jaxpr/psum | solution.py:209
  2391.1 56.0 %collective-permute-start.1 = (bf16[1,32,64,128]{3,1,2,0:T(8,128)(2,1)}, bf16[1,32,64,128]{3,1,2,0:T(8,128)(2,1)}, u32[]{:S(2)}, u32[]{:S(2)}) collective-permute-start(bf16[1,32,64,128]{3,1,2,0:T(8,128)(2,1)} %fusion.249), channel_id=1, source_target_pairs={{16,0},{17,1},{18,2},{19,3},{20,4},{21,5},{22,6},{23,7},{24,8},{25... | collective-permute-start | bytes 1572872 | tf_op jit(solution)/shard_map/while/body/eval_jaxpr/ppermute | solution.py:12
  2520.5 219.2 %all-reduce.22.cloned.1.call-start = ((), (), s32[]{:S(2)}) async-start(), calls=%async_computation | async-start | bytes 2359296 | tf_op jit(solution)/shard_map/while/body/eval_jaxpr/psum | solution.py:209
  2612.7 56.0 %collective-permute-start.1 = (bf16[1,32,64,128]{3,1,2,0:T(8,128)(2,1)}, bf16[1,32,64,128]{3,1,2,0:T(8,128)(2,1)}, u32[]{:S(2)}, u32[]{:S(2)}) collective-permute-start(bf16[1,32,64,128]{3,1,2,0:T(8,128)(2,1)} %fusion.249), channel_id=1, source_target_pairs={{16,0},{17,1},{18,2},{19,3},{20,4},{21,5},{22,6},{23,7},{24,8},{25... | collective-permute-start | bytes 1572872 | tf_op jit(solution)/shard_map/while/body/eval_jaxpr/ppermute | solution.py:12
  2742.2 219.1 %all-reduce.22.cloned.1.call-start = ((), (), s32[]{:S(2)}) async-start(), calls=%async_computation | async-start | bytes 2359296 | tf_op jit(solution)/shard_map/while/body/eval_jaxpr/psum | solution.py:209
  2834.3 56.0 %collective-permute-start.1 = (bf16[1,32,64,128]{3,1,2,0:T(8,128)(2,1)}, bf16[1,32,64,128]{3,1,2,0:T(8,128)(2,1)}, u32[]{:S(2)}, u32[]{:S(2)}) collective-permute-start(bf16[1,32,64,128]{3,1,2,0:T(8,128)(2,1)} %fusion.249), channel_id=1, source_target_pairs={{16,0},{17,1},{18,2},{19,3},{20,4},{21,5},{22,6},{23,7},{24,8},{25... | collective-permute-start | bytes 1572872 | tf_op jit(solution)/shard_map/while/body/eval_jaxpr/ppermute | solution.py:12
  (82 other events, 1161.3 us)
Sparse Core Ops, SparseCore 0:
  1075.4 112.8 all-reduce.21
  1297.0 112.8 all-reduce.21
  1518.7 112.7 all-reduce.21
  1740.3 112.8 all-reduce.21
  1962.0 112.7 all-reduce.21
  2183.6 112.8 all-reduce.21
  2405.3 112.7 all-reduce.21
  2626.8 112.8 all-reduce.21
  2848.5 112.7 all-reduce.21
where the time goes:
time: 2980 us; the launch traced here: 2970 us
  blocking collectives  1720 us (58%)
  waiting for transfers between devices  630 us (21%)
  other arithmetic  225 us (8%)
  local copies, waits for them, and re-layouts  212 us (7%)
  matrix products  137 us (5%)
  starting transfers between devices  30.5 us (1%)
    psum x18, blocking collectives, norm_back(): lax.psum((jnp.sum(grad_norm, axis=(0, 1, 2)), jnp.sum(grad_norm * normal_...  685 us
    psum x18, blocking collectives, moments(): lax.psum((jnp.sum(activ, axis=(0, 1, 2)), jnp.sum(activ * activ, axis=(0,...  681 us
    psum x9, waiting for transfers between devices, backward_tick(): lax.psum((local_parts[0], local_parts[1], local_parts[2], local_parts[3])...  630 us
    psum x9, blocking collectives, backward_tick(): lax.psum((local_parts[0], local_parts[1], local_parts[2], local_parts[3])...  352 us
    conv_general_dilated x36, matrix products, conv_apply(): lax.conv_general_dilated(pad_grid(field_in), kernel, (1, 1), 'VALID', dim...  69.3 us
    dot_general x162, matrix products, kernel_grad(): jnp.einsum('nhwc,nhwd->cd', window, grad_low, preferred_element_type=jnp....  68.2 us
    dynamic_update_slice x45, other arithmetic, put_slot(): lax.dynamic_update_index_in_dim(holder, jnp.where(usable, new_item, previ...  66.6 us
    dynamic_slice x45, local copies, waits for them, and re-layouts, put_slot(): previous = lax.dynamic_index_in_dim(holder, slot_pos, 0, keepdims=False)  61 us
  transfers between devices with their start and end apart: 27, of which 9 were waited for; matrix products, arithmetic and copies ran while one was open for 8% of the time, Pallas kernels for 0%

commit v1 on v0

v1 whole, which is shorter than its diff:
```python
import functools

import jax
import jax.numpy as jnp
from jax import lax
from jax.experimental import pallas as pl
from jax.experimental.pallas import tpu as pltpu
from jax.sharding import PartitionSpec as P

norm_eps = 1e-05
MESH = pl.DeviceIdType.MESH
bf16 = jnp.bfloat16
f32 = jnp.float32
C = 128
CHUNK = 2


def dot(a, b):
    return jnp.dot(a, b, preferred_element_type=f32)


def twice(v):
    return jnp.concatenate([v, v], axis=-1)


def fold_rows(v):
    one = jnp.sum(v, axis=0, keepdims=True)
    return one[:, :C] + one[:, C:]


def kernel(n, grp, *refs):
    (
        inp, cot, mean, std, w1, b1, g1, s1, w2, b2, g2, s2,
        bo, eg, gw1, gw2, gvec,
        XIN, COT, DY0, XC, LB, HS, DN, WF, WD, ACC, WR, PV, ST, VACC, VR,
        MSG, SLOT, GF, GS, GR0, GR1, GQ, GS2, GR2, GO,
        isem, wlsem, wssem, wrsem, msend, mrecv, olsem, ossem, orsem, gsend, grecv, vsem,
    ) = refs
    micro = inp.shape[0]
    half = micro // 2
    Q = inp.shape[1]
    W = inp.shape[3]
    rows = Q * W
    count = float(2 * rows * n)
    B = grp
    A = n // B
    PR = GF.shape[2]

    me = lax.axis_index("dp")
    sec = lax.axis_index("section")
    sib = 1 - sec
    ga = me // B
    gb = me % B

    barrier = pltpu.get_barrier_semaphore()

    def greet(i, carry):
        pl.semaphore_signal(barrier, inc=1, device_id={"dp": lax.rem(me + i, n)}, device_id_type=MESH)
        return carry

    lax.fori_loop(1, n, greet, 0)
    pl.semaphore_signal(barrier, inc=1, device_id={"section": sib}, device_id_type=MESH)

    for m in range(half):
        for e in range(2):
            lanes = pl.ds(e * C, C)
            pltpu.make_async_copy(inp.at[sec * half + m, :, e], XIN.at[m, :, :, lanes], isem.at[m]).start()
    for m in range(half):
        for e in range(2):
            lanes = pl.ds(e * C, C)
            pltpu.make_async_copy(cot.at[sec * half + m, :, e], COT.at[m, :, :, lanes], isem.at[half + m]).start()
    for v, ref in enumerate((w1, w2)):
        pltpu.make_async_copy(ref, WR.at[sec, v], wlsem.at[v]).start()

    for v, ref in enumerate((b1, g1, s1, b2, g2, s2)):
        PV[sec, v : v + 1] = ref[...]

    halo = jnp.zeros((W, C), bf16)
    for j in range(3):
        LB[j, 0, :, 0:C] = halo
        LB[j, Q, :, C : 2 * C] = halo

    def zero_halo(i, carry):
        XC[i, 0, :, 0:C] = halo
        XC[i, Q, :, C : 2 * C] = halo
        return carry

    lax.fori_loop(0, 4 * half, zero_halo, 0)
    for i in range(4):
        ACC[i] = jnp.zeros(ACC.shape[1:], f32)
    VACC[...] = jnp.zeros(VACC.shape, f32)
    GF[...] = jnp.zeros(GF.shape, f32)

    pl.semaphore_wait(barrier, n)

    for v in range(2):
        pltpu.make_async_copy(w1, WR.at[sec, v], wlsem.at[v]).wait()
    for v in range(2):
        pltpu.make_async_remote_copy(
            WR.at[sec, v], WR.at[sec, v], wssem.at[v], wrsem.at[v], device_id={"section": sib}, device_id_type=MESH
        ).start()
    pltpu.make_async_remote_copy(
        PV.at[sec], PV.at[sec], wssem.at[2], wrsem.at[2], device_id={"section": sib}, device_id_type=MESH
    ).start()

    def prep(b, v):
        for j in range(3):
            for t in range(2):
                for s in range(2):
                    for e in range(2):
                        i = 2 * t + s - e
                        r, c = slice(s * C, s * C + C), slice(e * C, e * C + C)
                        if 0 <= i <= 2:
                            WF[b * 2 + v, j, t, r, c] = (WR[b, v, i * 3 + j].astype(f32) * 0.5).astype(bf16)
                            WD[b * 2 + v, j, t, r, c] = WR[b, v, (2 - i) * 3 + 2 - j].T
                        else:
                            WF[b * 2 + v, j, t, r, c] = jnp.zeros((C, C), bf16)
                            WD[b * 2 + v, j, t, r, c] = jnp.zeros((C, C), bf16)

    def vec(b, v):
        return PV[b, v : v + 1]

    def send_sums(i, *sums):
        for r, v in enumerate(sums):
            MSG[i, r : r + 1] = v
        SLOT[i, me] = MSG[i]

        def one(d, carry):
            pltpu.make_async_remote_copy(
                MSG.at[i], SLOT.at[i, me], msend.at[i], mrecv.at[i],
                device_id={"dp": lax.rem(me + d, n)}, device_id_type=MESH,
            ).start()
            return carry

        lax.fori_loop(1, n, one, 0)

    def take_sums(i):
        if n > 1:
            many = SLOT.at[i, pl.ds(0, n - 1)]
            pltpu.make_async_copy(many, many, mrecv.at[i]).wait()
            pltpu.make_async_copy(many, many, msend.at[i]).wait()
        total = SLOT[i, 0]
        for d in range(1, n):
            total = total + SLOT[i, d]
        return total

    def norm_forward(b, v, m, total):
        mu = total[0:1] / count
        rstd = lax.rsqrt(total[1:2] / count - mu * mu + norm_eps)
        ST[b * 2 + v, m, 0:1] = mu
        ST[b * 2 + v, m, 1:2] = rstd
        sc = vec(b, 1 + 3 * v) * rstd
        return twice(sc), twice(vec(b, 2 + 3 * v) - mu * sc)

    def norm_backward(b, v, m, shift_sum, prod_sum):
        mu = ST[b * 2 + v, m, 0:1]
        rstd = ST[b * 2 + v, m, 1:2]
        gain_sum = rstd * (prod_sum - mu * shift_sum)
        VACC[b, 3 * v + 1 : 3 * v + 2] += gain_sum
        VACC[b, 3 * v + 2 : 3 * v + 3] += shift_sum
        ca = vec(b, 1 + 3 * v) * rstd
        cc = -ca * rstd * gain_sum / count
        cb = -ca * shift_sum / count - cc * mu
        return twice(ca), twice(cb), twice(cc)

    def put(center, q, v):
        k = v.shape[0]
        for j in range(3):
            u = (v if j == 1 else pltpu.roll(v, 1 if j == 0 else W - 1, 1)).astype(bf16)
            ref = center if j == 1 else LB.at[j]
            ref[q : q + k, :, C : 2 * C] = u[:, :, :C]
            ref[q + 1 : q + k + 1, :, 0:C] = u[:, :, C:]

    def get(center, q, k):
        return jnp.concatenate([center[q : q + k, :, C : 2 * C], center[q + 1 : q + k + 1, :, 0:C]], axis=-1)

    def conv(center, w):
        acc = None
        for j in range(3):
            ref = center if j == 1 else LB.at[j]
            for t in range(2):
                d = dot(ref[t : t + Q].reshape(rows, 2 * C), w[j, t])
                acc = d if acc is None else acc + d
        return acc

    def wgrad(i, center):
        left = jnp.concatenate([center[0:Q].reshape(rows, 2 * C), center[1 : Q + 1].reshape(rows, 2 * C)], axis=-1)
        right = jnp.concatenate([get(LB.at[j], 0, Q).reshape(rows, 2 * C) for j in range(3)], axis=-1)
        ACC[i] += lax.dot_general(left, right, (((0,), (0,)), ((), ())), preferred_element_type=f32)

    def chunks():
        return range(0, Q, CHUNK)

    def part(r, q):
        return r[q * W : (q + CHUNK) * W].reshape(CHUNK, W, 2 * C)

    def add8(total, v):
        return total + jnp.sum(v.reshape(-1, 8, 2 * C), axis=0)

    zero8 = jnp.zeros((8, 2 * C), f32)

    def act_of(h):
        return h + h * jnp.tanh(h)

    mean2 = twice(mean[...])
    inv2 = twice(1.0 / std[...])

    def standard(m, q):
        return (XIN[m, q : q + CHUNK].astype(f32) - mean2) * inv2

    def after_conv(b, v, m, r, cots):
        bias = twice(vec(b, 3 * v) * 0.5)
        t0, t1, t2, t3 = zero8, zero8, zero8, zero8
        for q in chunks():
            h = part(r, q) + bias
            HS[b * 2 + v, m, q : q + CHUNK] = h
            act = act_of(h)
            t0, t1 = add8(t0, act), add8(t1, act * act)
            if cots:
                dy = COT[m, q : q + CHUNK].astype(f32)
                t2, t3 = add8(t2, dy), add8(t3, dy * act)
        sums = (fold_rows(t0), fold_rows(t1))
        if cots:
            sums += (fold_rows(t2), fold_rows(t3))
        return sums

    def send_block(src, out, b, t, m, shifted):
        for e in range(2):
            lanes = pl.ds((1 - e) * C, C) if shifted else pl.ds(e * C, C)
            first = e if shifted else 0
            view = src.at[pl.ds(first, Q), :, lanes]
            dst = out.at[sec * half + m, :, e]

            @pl.when(sec == b)
            def _():
                pltpu.make_async_copy(view, dst, olsem.at[t]).start()

            @pl.when(sec != b)
            def _():
                pltpu.make_async_remote_copy(
                    view, dst, ossem.at[t], orsem.at[t], device_id={"section": sib}, device_id_type=MESH
                ).start()

    def wait_blocks(out, b, t):
        many = out.at[pl.ds(0, half)]

        @pl.when(sec == b)
        def _():
            pltpu.make_async_copy(many, many, olsem.at[t]).wait()
            pltpu.make_async_copy(many, many, orsem.at[t]).wait()

        @pl.when(sec != b)
        def _():
            pltpu.make_async_copy(many, many, ossem.at[t]).wait()

    def xc(b, v, m):
        return XC.at[(b * 2 + v) * half + m]

    def slot(stage, m):
        return (stage % 2) * half + m

    def stage0(m, carry):
        both = XIN.at[m]
        pltpu.make_async_copy(both, both, isem.at[m]).wait()
        center = xc(0, 0, m)
        for q in chunks():
            put(center, q, standard(m, q))
        send_sums(slot(0, m), *after_conv(0, 0, m, conv(center, WF.at[0]), False))
        return carry

    def stage_norm1(b, stage, m):
        sc, sh = norm_forward(b, 0, m, take_sums(slot(stage - 1, m)))
        center = xc(b, 1, m)
        for q in chunks():
            put(center, q, act_of(HS[b * 2, m, q : q + CHUNK]) * sc + sh)
        if b == 1:
            both = COT.at[m]
            pltpu.make_async_copy(both, both, isem.at[half + m]).wait()
        send_sums(slot(stage, m), *after_conv(b, 1, m, conv(center, WF.at[b * 2 + 1]), b == 1))

    def stage1(m, carry):
        stage_norm1(0, 1, m)
        return carry

    def stage2(m, carry):
        sc, sh = norm_forward(0, 1, m, take_sums(slot(1, m)))
        center = xc(1, 0, m)
        for q in chunks():
            put(center, q, standard(m, q) + (act_of(HS[1, m, q : q + CHUNK]) * sc + sh))
        send_block(center, bo, 0, 0, m, True)
        send_sums(slot(2, m), *after_conv(1, 0, m, conv(center, WF.at[2]), False))
        return carry

    def stage3(m, carry):
        stage_norm1(1, 3, m)
        return carry

    def back_chunk(i, m, q, dy, coef):
        ca, cb, cc = coef
        h = HS[i, m, q : q + CHUNK]
        u = 1.0 + jnp.tanh(h)
        act = h * u
        dp = (ca * dy + (cc * act + cb)) * (act + (0.5 * u) * (1.0 - act))
        put(LB.at[1], q, dp)
        return act, dp

    def stage_e(b, stage, m):
        total = take_sums(slot(stage - 1, m))
        if b == 1:
            sc, sh = norm_forward(1, 1, m, total)
            coef = norm_backward(1, 1, m, total[2:3], total[3:4])
        else:
            coef = norm_backward(0, 1, m, total[0:1], total[1:2])
            VACC[1, 0:1] += total[2:3]
        t0, t1, t2 = zero8, zero8, zero8
        for q in chunks():
            dy = (COT if b == 1 else DY0)[m, q : q + CHUNK].astype(f32)
            act, dp = back_chunk(b * 2 + 1, m, q, dy, coef)
            t2 = add8(t2, dp)
            if b == 1:
                final = get(xc(1, 0, m), q, CHUNK).astype(f32) + (act * sc + sh)
                XIN[m, q : q + CHUNK] = final.astype(bf16)
        if b == 1:
            send_block(XIN.at[m], bo, 1, 1, m, False)
        r = conv(LB.at[1], WD.at[b * 2 + 1])
        for q in chunks():
            dn = part(r, q)
            DN[m, q : q + CHUNK] = dn
            t0, t1 = add8(t0, dn), add8(t1, dn * act_of(HS[b * 2, m, q : q + CHUNK]))
        send_sums(slot(stage, m), fold_rows(t0), fold_rows(t1), fold_rows(t2))
        wgrad(b * 2 + 1, xc(b, 1, m))

    def stage4(m, carry):
        stage_e(1, 4, m)
        return carry

    def coef_f(b, stage, m):
        total = take_sums(slot(stage - 1, m))
        VACC[b, 3:4] += total[2:3]
        return norm_backward(b, 0, m, total[0:1], total[1:2])

    def low_f(b, m, coef):
        t2 = zero8
        for q in chunks():
            t2 = add8(t2, back_chunk(b * 2, m, q, DN[m, q : q + CHUNK], coef)[1])
        return t2

    def stage5(m, carry):
        t2 = low_f(1, m, coef_f(1, 5, m))
        r = conv(LB.at[1], WD.at[2])
        t0, t1 = zero8, zero8
        for q in chunks():
            da = (COT[m, q : q + CHUNK].astype(f32) + part(r, q)).astype(bf16)
            DY0[m, q : q + CHUNK] = da
            da = da.astype(f32)
            t0, t1 = add8(t0, da), add8(t1, da * act_of(HS[1, m, q : q + CHUNK]))
        send_sums(slot(5, m), fold_rows(t0), fold_rows(t1), fold_rows(t2))
        send_block(DY0.at[m], eg, 1, 2, m, False)
        wgrad(2, xc(1, 0, m))
        return carry

    def taps(b, v):
        a = ACC.at[b * 2 + v]
        for i in range(3):
            for j in range(3):
                out = None
                for t in range(2):
                    for s in range(2):
                        e = 2 * t + s - i
                        if 0 <= e <= 1:
                            r = (2 * t + s) * C
                            c = ((2 - j) * 2 + e) * C
                            d = a[r : r + C, c : c + C]
                            out = d if out is None else out + d
                yield (v * 9 + i * 3 + j) * C, out

    flat = A * PR

    def pieces(row, size):
        while size > 0:
            p, o = row // PR, row % PR
            k = min(size, PR - o)
            yield p // A, p % A, o, k
            row, size = row + k, size - k

    def phase0(b, x):
        for v in range(2):
            for row, val in taps(b, v):
                at = 0
                for pb, pa, o, k in pieces(row, C):
                    GF[pb, pa, o : o + k] = val[at : at + k]
                    at += k

        @pl.when(sec != b)
        def _():
            GS[...] = GF[...].astype(bf16)
            pltpu.make_async_remote_copy(
                GS, GR0, gsend.at[x, 0], grecv.at[x, 0], device_id={"section": sib}, device_id_type=MESH
            ).start()
            pltpu.make_async_copy(GS, GS, gsend.at[x, 0]).wait()

    def phase1(b, x):
        @pl.when(sec == b)
        def _():
            pltpu.make_async_copy(GR0, GR0, grecv.at[x, 0]).wait()
            GF[...] += GR0[...].astype(f32)
            GS[...] = GF[...].astype(bf16)
            GR1[gb] = GS[gb]
            for d in range(1, B):
                to = lax.rem(gb + d, B)
                pltpu.make_async_remote_copy(
                    GS.at[to], GR1.at[gb], gsend.at[x, 1], grecv.at[x, 1],
                    device_id={"dp": ga * B + to}, device_id_type=MESH,
                ).start()

    def group_wait(ref, size, x, p):
        if size > 1:
            many = ref.at[pl.ds(0, size - 1)]
            pltpu.make_async_copy(many, many, grecv.at[x, p]).wait()
            pltpu.make_async_copy(many, many, gsend.at[x, p]).wait()

    def phase2(b, x):
        @pl.when(sec == b)
        def _():
            group_wait(GR1, B, x, 1)
            total = GR1[0].astype(f32)
            for d in range(1, B):
                total = total + GR1[d].astype(f32)
            GQ[...] = total
            GS2[...] = total.astype(bf16)
            GR2[ga] = GS2[ga]
            for d in range(1, A):
                to = lax.rem(ga + d, A)
                pltpu.make_async_remote_copy(
                    GS2.at[to], GR2.at[ga], gsend.at[x, 2], grecv.at[x, 2],
                    device_id={"dp": to * B + gb}, device_id_type=MESH,
                ).start()

    def phase3(b, x):
        @pl.when(sec == b)
        def _():
            group_wait(GR2, A, x, 2)
            total = GR2[0].astype(f32)
            for d in range(1, A):
                total = total + GR2[d].astype(f32)
            GO[gb, ga] = total.astype(bf16)
            for d in range(1, A):
                pltpu.make_async_remote_copy(
                    GO.at[gb, ga], GO.at[gb, ga], gsend.at[x, 3], grecv.at[x, 3],
                    device_id={"dp": lax.rem(ga + d, A) * B + gb}, device_id_type=MESH,
                ).start()

    def phase4(b, x):
        @pl.when(sec == b)
        def _():
            group_wait(GO.at[gb], A, x, 3)
            for d in range(1, B):
                pltpu.make_async_remote_copy(
                    GO.at[gb], GO.at[gb], gsend.at[x, 4], grecv.at[x, 4],
                    device_id={"dp": ga * B + lax.rem(gb + d, B)}, device_id_type=MESH,
                ).start()

    def phase5(b, x):
        @pl.when(sec == b)
        def _():
            group_wait(GO, B, x, 4)
            for v, out in enumerate((gw1, gw2)):
                for k in range(9):
                    at = 0
                    for pb, pa, o, size in pieces((v * 9 + k) * C, C):
                        out[k, at : at + size] = GO[pb, pa, o : o + size].astype(f32)
                        at += size

    @pl.when(sec != 0)
    def _():
        pltpu.make_async_copy(WR.at[0, 0], WR.at[0, 0], wrsem.at[0]).wait()

    prep(0, 0)
    pltpu.make_async_copy(PV.at[0], PV.at[0], wrsem.at[2]).wait()

    @pl.when(sec == 0)
    def _():
        pltpu.make_async_copy(WR.at[0, 0], WR.at[0, 0], wrsem.at[0]).wait()

    lax.fori_loop(0, half, stage0, 0)
    pltpu.make_async_copy(WR.at[0, 1], WR.at[0, 1], wrsem.at[1]).wait()
    for v in range(2):
        pltpu.make_async_copy(WR.at[0, 0], WR.at[0, 0], wssem.at[v]).wait()
    pltpu.make_async_copy(PV.at[0], PV.at[0], wssem.at[2]).wait()
    prep(0, 1)
    lax.fori_loop(0, half, stage1, 0)
    prep(1, 0)
    lax.fori_loop(0, half, stage2, 0)
    prep(1, 1)
    lax.fori_loop(0, half, stage3, 0)
    lax.fori_loop(0, half, stage4, 0)
    lax.fori_loop(0, half, stage5, 0)
    phase0(1, 0)

    def stage6(m, carry):
        stage_e(0, 6, m)

        @pl.when(m == 1)
        def _():
            phase1(1, 0)

        @pl.when(m == half - 1)
        def _():
            phase2(1, 0)

        return carry

    lax.fori_loop(0, half, stage6, 0)

    def stage7(m, carry):
        t2 = low_f(0, m, coef_f(0, 7, m))
        send_sums(slot(7, m), fold_rows(t2))
        wgrad(0, xc(0, 0, m))

        @pl.when(m == 1)
        def _():
            phase3(1, 0)

        @pl.when(m == half - 1)
        def _():
            phase4(1, 0)

        return carry

    lax.fori_loop(0, half, stage7, 0)
    phase0(0, 1)

    def stage8(m, carry):
        mu = ST[0, m, 0:1]
        rstd = ST[0, m, 1:2]
        total = SLOT[slot(6, m), 0]
        for d in range(1, n):
            total = total + SLOT[slot(6, m), d]
        gain_sum = rstd * (total[1:2] - mu * total[0:1])
        ca = vec(0, 1) * rstd
        cc = -ca * rstd * gain_sum / count
        cb = -ca * total[0:1] / count - cc * mu
        low_f(0, m, (twice(ca), twice(cb), twice(cc)))
        r = conv(LB.at[1], WD.at[0])
        for q in chunks():
            da = (DY0[m, q : q + CHUNK].astype(f32) + part(r, q)) * inv2
            COT[m, q : q + CHUNK] = da.astype(bf16)
        send_block(COT.at[m], eg, 0, 3, m, False)

        @pl.when(m == 0)
        def _():
            phase5(1, 0)
            phase1(0, 1)

        @pl.when(m == 2)
        def _():
            phase2(0, 1)

        @pl.when(m == half - 1)
        def _():
            phase3(0, 1)

        return carry

    lax.fori_loop(0, half, stage8, 0)

    for m in range(half):
        VACC[0, 0:1] += take_sums(slot(7, m))[0:1]
    pltpu.make_async_remote_copy(
        VACC.at[sib], VR, vsem.at[0], vsem.at[1], device_id={"section": sib}, device_id_type=MESH
    ).start()
    phase4(0, 1)
    pltpu.make_async_copy(VR, VR, vsem.at[1]).wait()
    pltpu.make_async_copy(VR, VR, vsem.at[0]).wait()
    gvec[...] = VACC[sec] + VR[...]
    phase5(0, 1)
    wait_blocks(bo, 0, 0)
    wait_blocks(bo, 1, 1)
    wait_blocks(eg, 1, 2)
    wait_blocks(eg, 0, 3)


def group_of(n):
    return min(d for d in range(1, n + 1) if n % d == 0 and d * d >= n)


def solution(mesh):
    n = mesh.shape["dp"]
    grp = group_of(n)

    def per_device(inputs, channel_mean, channel_std, cotangent, conv_w1, conv_b1, bn_gain1, bn_shift1, conv_w2, conv_b2, bn_gain2, bn_shift2):
        micro, _, H, W, _ = inputs.shape
        half = micro // 2
        Q = H // 2
        rows = Q * W
        field = (micro, Q, 2, W, C)
        piece = -(-18 * C // n // 16) * 16
        anywhere = pl.BlockSpec(memory_space=pl.ANY)
        vmem = pl.BlockSpec(memory_space=pltpu.VMEM)
        D = pltpu.SemaphoreType.DMA
        V = pltpu.VMEM
        out = pl.pallas_call(
            functools.partial(kernel, n, grp),
            out_shape=[
                jax.ShapeDtypeStruct(field, bf16),
                jax.ShapeDtypeStruct(field, bf16),
                jax.ShapeDtypeStruct((9, C, C), f32),
                jax.ShapeDtypeStruct((9, C, C), f32),
                jax.ShapeDtypeStruct((8, C), f32),
            ],
            in_specs=[anywhere, anywhere, vmem, vmem, anywhere, vmem, vmem, vmem, anywhere, vmem, vmem, vmem],
            out_specs=[anywhere, anywhere, vmem, vmem, vmem],
            scratch_shapes=[
                V((half, Q, W, 2 * C), bf16),
                V((half, Q, W, 2 * C), bf16),
                V((half, Q, W, 2 * C), bf16),
                V((4 * half, Q + 1, W, 2 * C), bf16),
                V((3, Q + 1, W, 2 * C), bf16),
                V((4, half, Q, W, 2 * C), f32),
                V((half, Q, W, 2 * C), f32),
                V((4, 3, 2, 2 * C, 2 * C), bf16),
                V((4, 3, 2, 2 * C, 2 * C), bf16),
                V((4, 4 * C, 6 * C), f32),
                V((2, 2, 9, C, C), bf16),
                V((2, 8, C), f32),
                V((4, half, 8, C), f32),
                V((2, 8, C), f32),
                V((8, C), f32),
                V((2 * half, 4, C), f32),
                V((2 * half, n, 4, C), f32),
                V((grp, n // grp, piece, C), f32),
                V((grp, n // grp, piece, C), bf16),
                V((grp, n // grp, piece, C), bf16),
                V((grp, n // grp, piece, C), bf16),
                V((n // grp, piece, C), f32),
                V((n // grp, piece, C), bf16),
                V((n // grp, piece, C), bf16),
                V((grp, n // grp, piece, C), bf16),
                D((2 * half,)),
                D((2,)),
                D((3,)),
                D((3,)),
                D((2 * half,)),
                D((2 * half,)),
                D((4,)),
                D((4,)),
                D((4,)),
                D((2, 5)),
                D((2, 5)),
                D((2,)),
            ],
            compiler_params=pltpu.CompilerParams(
                collective_id=0, has_side_effects=True, vmem_limit_bytes=62 * 2**20
            ),
        )(
            inputs.reshape(field),
            cotangent.reshape(field),
            channel_mean[None],
            channel_std[None],
            conv_w1.reshape(9, C, C),
            conv_b1,
            bn_gain1,
            bn_shift1,
            conv_w2.reshape(9, C, C),
            conv_b2,
            bn_gain2,
            bn_shift2,
        )
        bo, eg, gw1, gw2, gvec = out
        whole = (1, micro, 1, H, W, C)
        return (
            bo.reshape(whole),
            eg.reshape(whole),
            gw1.reshape(1, 3, 3, C, C),
            gvec[0:1],
            gvec[1:2],
            gvec[2:3],
            gw2.reshape(1, 3, 3, C, C),
            gvec[3:4],
            gvec[4:5],
            gvec[5:6],
        )

    in_specs = (
        P(None, "dp", None, None, None),
        P(),
        P(),
        P(None, "dp", None, None, None),
        P("section", None, None, None, None),
        P("section", None),
        P("section", None),
        P("section", None),
        P("section", None, None, None, None),
        P("section", None),
        P("section", None),
        P("section", None),
    )
    out_specs = (
        P("section", None, "dp", None, None, None),
        P("section", None, "dp", None, None, None),
        P("section", None, None, None, None),
        P("section", None),
        P("section", None),
        P("section", None),
        P("section", None, None, None, None),
        P("section", None),
        P("section", None),
        P("section", None),
    )
    return jax.shard_map(per_device, mesh=mesh, in_specs=in_specs, out_specs=out_specs, check_vma=False)
```

time: 2980 us -> 134 us (0.04)
  blocking collectives: 1720 us -> 0 us
  waiting for transfers between devices: 630 us -> 0 us
  other arithmetic: 225 us -> 0 us
  local copies, waits for them, and re-layouts: 212 us -> 10.5 us
  matrix products: 137 us -> 0 us
  Pallas kernels: 0 us -> 123 us
  starting transfers between devices: 30.5 us -> 0 us
    psum x45 -> x0, blocking collectives: 1720 us -> none  [the longest x18 685 us: norm_back(): lax.psum((jnp.sum(grad_norm, axis=(0, 1, 2)), jnp.sum(grad_norm * normal_...]
    psum x9 -> x0, waiting for transfers between devices: 630 us -> none  [backward_tick(): lax.psum((local_parts[0], local_parts[1], local_parts[2], local_parts[3])...]
    pallas_call x0 -> x1, Pallas kernels: none -> 123 us  [per_device(): pl.pallas_call(functools.partial(kernel, n, grp), out_shape=[jax.ShapeDty...]
    dynamic_slice x108 -> x0, local copies, waits for them, and re-layouts: 104 us -> none  [the longest x45 61 us: put_slot(): previous = lax.dynamic_index_in_dim(holder, slot_pos, 0, keepdims=False)]
    conv_general_dilated x36 -> x0, matrix products: 69.3 us -> none  [conv_apply(): lax.conv_general_dilated(pad_grid(field_in), kernel, (1, 1), 'VALID', dim...]
    dot_general x162 -> x0, matrix products: 68.2 us -> none  [kernel_grad(): jnp.einsum('nhwc,nhwd->cd', window, grad_low, preferred_element_type=jnp....]
    reduce_sum x36 -> x0, other arithmetic: 67.9 us -> none  [the longest x9 19.4 us: backward_block(): jnp.sum(grad_pre_two, axis=(0, 1, 2))]
    dynamic_update_slice x45 -> x0, other arithmetic: 66.6 us -> none  [put_slot(): lax.dynamic_update_index_in_dim(holder, jnp.where(usable, new_item, previ...]
  transfers between devices with their start and end apart: 27 -> 0, of which waited for: 9 -> 0; matrix products, arithmetic and copies ran while one was open for 8% -> 0% of each run, Pallas kernels for 0% -> 0%
where the time goes in v1:
time: 134 us
  Pallas kernels  123 us (92%)
  local copies, waits for them, and re-layouts  10.5 us (8%)
    pallas_call x1, Pallas kernels, per_device(): pl.pallas_call(functools.partial(kernel, n, grp), out_shape=[jax.ShapeDty...  123 us
    unnamed x10, local copies, waits for them, and re-layouts  9.07 us

profile of v1, /device:TPU:0, one launch (start us, length us, event | category | flops | bytes accessed | tf_op | source)
XLA Modules:
  0.0 134.0 jit_solution(8993560383424629471)
XLA Ops:
  0.6 122.8 %shard_map.195 = (bf16[8,16,2,64,128]{4,3,2,1,0:T(8,128)(2,1)}, bf16[8,16,2,64,128]{4,3,2,1,0:T(8,128)(2,1)}, f32[9,128,128]{2,1,0:T(8,128)}, f32[9,128,128]{2,1,0:T(8,128)}, f32[8,128]{1,0:T(8,128)}) custom-call(bf16[8,16,2,64,128]{4,3,2,1,0:T(8,128)(2,1)} %bitcast.14, bf16[8,16,2,64,128]{4,3,2,1,0:T(8,128)(2,1)} %bitcast.15, f32[1,128]{1,0:T(1,128)} %bitcast.22, ...), custom_call_target="tpu_custom_call" | custom-call | tf_op jit(solution)/shard_map/pallas_call | solution.py:602
  123.5 1.4 %fusion = (f32[1,128]{1,0:T(1,128)}, f32[1,128]{1,0:T(1,128)}, f32[1,128]{1,0:T(1,128)}, f32[1,128]{1,0:T(1,128)}, f32[1,128]{1,0:T(1,128)}, /*index=5*/f32[1,128]{1,0:T(1,128)}) fusion(f32[8,128]{1,0:T(8,128)} %get-tuple-element.18), kind=kLoop, calls=%fused_computation | loop fusion | bytes 6144 | tf_op jit(solution)/shard_map/slice | solution.py:681
  124.9 0.0 copy-start
  124.9 5.4 %copy.28 = bf16[1,8,1,32,64,128]{5,4,3,2,1,0:T(8,128)(2,1)} copy(bf16[1,8,1,32,64,128]{5,4,3,2,1,0:T(8,128)(2,1)} %bitcast.17) | data formatting | bytes 8388608
  130.3 0.0 copy-done
  130.3 0.0 copy-start.2
  130.3 0.0 copy-start.1
  130.4 2.0 %copy.29 = bf16[1,8,1,32,64,128]{5,4,3,2,1,0:T(8,128)(2,1)} copy(bf16[1,8,1,32,64,128]{5,4,3,2,1,0:T(8,128)(2,1)S(1)} %bitcast.16) | data formatting | bytes 8388608
  132.4 0.0 copy-done.2
  132.4 0.8 copy.30
  133.2 0.0 copy-done.1
  133.2 0.8 copy.31
Async XLA Ops:
  124.9 5.4 %copy-start = (bf16[8,16,2,64,128]{4,3,2,1,0:T(8,128)(2,1)S(1)}, bf16[8,16,2,64,128]{4,3,2,1,0:T(8,128)(2,1)}, u32[]{:S(2)}) copy-start(bf16[8,16,2,64,128]{4,3,2,1,0:T(8,128)(2,1)} %get-tuple-element.16) | copy-start | bytes 12582916
  130.3 2.0 %copy-start.2 = (f32[9,128,128]{2,1,0:T(8,128)S(1)}, f32[9,128,128]{2,1,0:T(8,128)}, u32[]{:S(2)}) copy-start(f32[9,128,128]{2,1,0:T(8,128)} %get-tuple-element.17) | copy-start | bytes 1769476
  130.3 2.8 %copy-start.1 = (f32[9,128,128]{2,1,0:T(8,128)S(1)}, f32[9,128,128]{2,1,0:T(8,128)}, u32[]{:S(2)}) copy-start(f32[9,128,128]{2,1,0:T(8,128)} %get-tuple-element.19) | copy-start | bytes 1769476

commit v2 on v1

v2 whole, which is shorter than its diff:
```python
import functools

import jax
import jax.numpy as jnp
from jax import lax
from jax.experimental import pallas as pl
from jax.experimental.pallas import tpu as pltpu
from jax.sharding import PartitionSpec as P

norm_eps = 1e-05
MESH = pl.DeviceIdType.MESH
bf16 = jnp.bfloat16
f32 = jnp.float32
C = 128
CHUNK = 2
VMEM_LIMIT = 52 * 2**20


def dot(a, b):
    return jnp.dot(a, b, preferred_element_type=f32)


def twice(v):
    return jnp.concatenate([v, v], axis=-1)


def fold_rows(v):
    one = jnp.sum(v, axis=0, keepdims=True)
    return one[:, :C] + one[:, C:]


def piece_rows(rows, n):
    size = -(-rows // n // 16) * 16
    return size, -(-rows // size)


def kernel(n, *refs):
    (
        inp, cot, mean, std, w1, b1, g1, s1, w2, b2, g2, s2,
        bo, eg, GO2, GO1, gvec,
        XIN, COT, XC, LB, HS, WF, WD, ACC, WR, PV, ST, VACC, VR,
        MSG, SLOT, GS2, GS1, GR2, GR1, GP2, GP1,
        isem, wlsem, wssem, wrsem, msend, mrecv, olsem, ossem, orsem, gsend, grecv, vsem,
    ) = refs
    micro = inp.shape[0]
    half = micro // 2
    Q = inp.shape[1]
    W = inp.shape[3]
    rows = Q * W
    count = float(2 * rows * n)

    me = lax.axis_index("dp")
    sec = lax.axis_index("section")
    sib = 1 - sec

    def peer(d):
        return {"dp": lax.rem(me + d, n)}

    def every_peer(body):
        if n <= 16:
            for d in range(1, n):
                body(d)
        else:
            lax.fori_loop(1, n, lambda d, carry: (body(d), carry)[1], 0)

    def wait(ref, sem):
        pltpu.make_async_copy(ref, ref, sem).wait()

    def to_sibling(src, dst, send, recv):
        pltpu.make_async_remote_copy(
            src, dst, send, recv, device_id={"section": sib}, device_id_type=MESH
        ).start()

    barrier = pltpu.get_barrier_semaphore()
    pl.semaphore_signal(barrier, inc=1, device_id={"section": sib}, device_id_type=MESH)
    every_peer(lambda d: pl.semaphore_signal(barrier, inc=1, device_id=peer(d), device_id_type=MESH))

    for v, ref in enumerate((w1, w2)):
        pltpu.make_async_copy(ref, WR.at[sec, v], wlsem.at[v]).start()
    for src, dst, at in ((inp, XIN, 0), (cot, COT, half)):
        for m in range(half):
            for e in range(2):
                pltpu.make_async_copy(
                    src.at[sec * half + m, :, e], dst.at[m, :, :, pl.ds(e * C, C)], isem.at[at + m]
                ).start()

    for v, ref in enumerate((b1, g1, s1, b2, g2, s2)):
        PV[sec, v : v + 1] = ref[...]

    halo = jnp.zeros((W, C), bf16)
    for j in range(2):
        LB[j, 0, :, 0:C] = halo
        LB[j, Q, :, C : 2 * C] = halo

    def zero_halo(i, carry):
        XC[i, 0, :, 0:C] = halo
        XC[i, Q, :, C : 2 * C] = halo
        return carry

    lax.fori_loop(0, 4 * half + 1, zero_halo, 0)
    empty = jnp.zeros((C, C), bf16)
    for i in range(4):
        ACC[i] = jnp.zeros(ACC.shape[1:], f32)
        for j in range(3):
            for ref in (WF, WD):
                ref[i, j, 0, 0:C, C : 2 * C] = empty
                ref[i, j, 1, C : 2 * C, 0:C] = empty
    VACC[...] = jnp.zeros(VACC.shape, f32)
    GS2[...] = jnp.zeros(GS2.shape, bf16)
    GS1[...] = jnp.zeros(GS1.shape, bf16)

    pl.semaphore_wait(barrier, n)

    to_sibling(PV.at[sec], PV.at[sec], wssem.at[2], wrsem.at[2])
    for v in range(2):
        wait(WR.at[sec, v], wlsem.at[v])
        to_sibling(WR.at[sec, v], WR.at[sec, v], wssem.at[v], wrsem.at[v])

    def blocks():
        for j in range(3):
            for t in range(2):
                for s in range(2):
                    for e in range(2):
                        i = 2 * t + s - e
                        if 0 <= i <= 2:
                            yield i, j, t, slice(s * C, s * C + C), slice(e * C, e * C + C)

    def prep_forward(b, v):
        for i, j, t, r, c in blocks():
            WF[b * 2 + v, j, t, r, c] = (WR[b, v, i * 3 + j].astype(f32) * 0.5).astype(bf16)

    def prep_backward(b, v):
        for i, j, t, r, c in blocks():
            WD[b * 2 + v, j, t, r, c] = WR[b, v, (2 - i) * 3 + 2 - j].T

    def vec(b, v):
        return PV[b, v : v + 1]

    def send_sums(i, *sums):
        for r, v in enumerate(sums):
            MSG[i, r : r + 1] = v
        SLOT[i, me] = MSG[i]
        every_peer(
            lambda d: pltpu.make_async_remote_copy(
                MSG.at[i], SLOT.at[i, me], msend.at[i], mrecv.at[i], device_id=peer(d), device_id_type=MESH
            ).start()
        )

    def sum_slots(i):
        total = SLOT[i, 0]
        for d in range(1, n):
            total = total + SLOT[i, d]
        return total

    def take_sums(i):
        if n > 1:
            many = SLOT.at[i, pl.ds(0, n - 1)]
            wait(many, mrecv.at[i])
            wait(many, msend.at[i])
        return sum_slots(i)

    def norm_forward(b, v, m, total):
        mu = total[0:1] / count
        rstd = lax.rsqrt(total[1:2] / count - mu * mu + norm_eps)
        ST[b * 2 + v, m, 0:1] = mu
        ST[b * 2 + v, m, 1:2] = rstd
        sc = vec(b, 1 + 3 * v) * rstd
        return twice(sc), twice(vec(b, 2 + 3 * v) - mu * sc)

    def norm_backward(b, v, m, shift_sum, prod_sum):
        mu = ST[b * 2 + v, m, 0:1]
        rstd = ST[b * 2 + v, m, 1:2]
        gain_sum = rstd * (prod_sum - mu * shift_sum)
        VACC[b, 3 * v + 1 : 3 * v + 2] += gain_sum
        VACC[b, 3 * v + 2 : 3 * v + 3] += shift_sum
        ca = vec(b, 1 + 3 * v) * rstd
        cc = -ca * rstd * gain_sum / count
        cb = -ca * shift_sum / count - cc * mu
        return twice(ca), twice(cb), twice(cc)

    def put(trio, q, v):
        k = v.shape[0]
        for j, ref in enumerate(trio):
            u = (v if j == 1 else pltpu.roll(v, 1 if j == 0 else W - 1, 1)).astype(bf16)
            ref[q : q + k, :, C : 2 * C] = u[:, :, :C]
            ref[q + 1 : q + k + 1, :, 0:C] = u[:, :, C:]

    def get(center, q, k):
        return jnp.concatenate([center[q : q + k, :, C : 2 * C], center[q + 1 : q + k + 1, :, 0:C]], axis=-1)

    def conv(trio, w):
        acc = None
        for j, ref in enumerate(trio):
            for t in range(2):
                d = dot(ref[t : t + Q].reshape(rows, 2 * C), w[j, t])
                acc = d if acc is None else acc + d
        return acc

    def wgrad(i, center, trio, which=(0, 1, 2)):
        left = jnp.concatenate([center[0:Q].reshape(rows, 2 * C), center[1 : Q + 1].reshape(rows, 2 * C)], axis=-1)
        for j in which:
            right = get(trio[j], 0, Q).reshape(rows, 2 * C)
            ACC[i, :, j * 2 * C : (j + 1) * 2 * C] += lax.dot_general(
                left, right, (((0,), (0,)), ((), ())), preferred_element_type=f32
            )

    def chunks():
        return range(0, Q, CHUNK)

    def part(r, q):
        return r[q * W : (q + CHUNK) * W].reshape(CHUNK, W, 2 * C)

    def add8(total, v):
        return total + jnp.sum(v.reshape(-1, 8, 2 * C), axis=0)

    zero8 = jnp.zeros((8, 2 * C), f32)

    def act_of(h):
        return h + h * jnp.tanh(h)

    mean2 = twice(mean[...])
    inv2 = twice(1.0 / std[...])

    def standard(m, q):
        return (XIN[m, q : q + CHUNK].astype(f32) - mean2) * inv2

    def after_conv(b, v, m, r, cots):
        bias = twice(vec(b, 3 * v) * 0.5)
        t0, t1, t2, t3 = zero8, zero8, zero8, zero8
        for q in chunks():
            h = part(r, q) + bias
            HS[b * 2 + v, m, q : q + CHUNK] = h
            act = act_of(h)
            t0, t1 = add8(t0, act), add8(t1, act * act)
            if cots:
                dy = COT[m, q : q + CHUNK].astype(f32)
                t2, t3 = add8(t2, dy), add8(t3, dy * act)
        sums = (fold_rows(t0), fold_rows(t1))
        if cots:
            sums += (fold_rows(t2), fold_rows(t3))
        return sums

    def send_block(views, b, t):
        @pl.when(sec == b)
        def _():
            for src, dst in views:
                pltpu.make_async_copy(src, dst, olsem.at[t]).start()

        @pl.when(sec != b)
        def _():
            for src, dst in views:
                to_sibling(src, dst, ossem.at[t], orsem.at[t])

    def sent_blocks(out, b, t):
        many = out.at[pl.ds(0, half)]

        @pl.when(sec == b)
        def _():
            wait(many, olsem.at[t])

        @pl.when(sec != b)
        def _():
            wait(many, ossem.at[t])

    def came_blocks(out, b, t):
        @pl.when(sec == b)
        def _():
            wait(out.at[pl.ds(0, half)], orsem.at[t])

    def xc(b, v, m):
        return XC.at[(b * 2 + v) * half + m]

    def trio_of(center):
        return LB.at[0], center, LB.at[1]

    low = trio_of(XC.at[4 * half])

    def slot(stage, m):
        return (stage % 2) * half + m

    def stage0(m, carry):
        wait(XIN.at[m], isem.at[m])
        trio = trio_of(xc(0, 0, m))
        for q in chunks():
            put(trio, q, standard(m, q))
        send_sums(slot(0, m), *after_conv(0, 0, m, conv(trio, WF.at[0]), False))
        return carry

    def stage_norm1(b, stage, m):
        sc, sh = norm_forward(b, 0, m, take_sums(slot(stage - 1, m)))
        if b == 1:
            wait(COT.at[m], isem.at[half + m])
        trio = trio_of(xc(b, 1, m))
        for q in chunks():
            put(trio, q, act_of(HS[b * 2, m, q : q + CHUNK]) * sc + sh)
        send_sums(slot(stage, m), *after_conv(b, 1, m, conv(trio, WF.at[b * 2 + 1]), b == 1))

    def stage1(m, carry):
        stage_norm1(0, 1, m)
        return carry

    def stage2(m, carry):
        sc, sh = norm_forward(0, 1, m, take_sums(slot(1, m)))
        center = xc(1, 0, m)
        trio = trio_of(center)
        for q in chunks():
            put(trio, q, standard(m, q) + (act_of(HS[1, m, q : q + CHUNK]) * sc + sh))
        send_sums(slot(2, m), *after_conv(1, 0, m, conv(trio, WF.at[2]), False))
        send_block(
            [
                (center.at[pl.ds(e, Q), :, pl.ds((1 - e) * C, C)], bo.at[sec * half + m, :, :, pl.ds(e * C, C)])
                for e in range(2)
            ],
            0,
            0,
        )
        return carry

    def stage3(m, carry):
        stage_norm1(1, 3, m)
        return carry

    def back_chunk(trio, i, m, q, dy, coef):
        ca, cb, cc = coef
        h = HS[i, m, q : q + CHUNK]
        u = 1.0 + jnp.tanh(h)
        act = h * u
        dp = (ca * dy + (cc * act + cb)) * (act + (0.5 * u) * (1.0 - act))
        put(trio, q, dp)
        return act, dp

    def stage_e(b, stage, m):
        total = take_sums(slot(stage - 1, m))
        if b == 1:
            sc, sh = norm_forward(1, 1, m, total)
            coef = norm_backward(1, 1, m, total[2:3], total[3:4])
        else:
            coef = norm_backward(0, 1, m, total[0:1], total[1:2])
            VACC[1, 0:1] += total[2:3]
        t0, t1, t2 = zero8, zero8, zero8
        i = b * 2 + 1
        for q in chunks():
            dy = COT[m, q : q + CHUNK].astype(f32)
            act, dp = back_chunk(low, i, m, q, dy, coef)
            t2 = add8(t2, dp)
            if b == 1:
                final = get(xc(1, 0, m), q, CHUNK).astype(f32) + (act * sc + sh)
                XIN[m, q : q + CHUNK] = final.astype(bf16)
        r = conv(low, WD.at[i])
        wgrad(i, xc(b, 1, m), low)
        for q in chunks():
            dn = part(r, q)
            HS[i, m, q : q + CHUNK] = dn
            t0, t1 = add8(t0, dn), add8(t1, dn * act_of(HS[b * 2, m, q : q + CHUNK]))
        send_sums(slot(stage, m), fold_rows(t0), fold_rows(t1), fold_rows(t2))
        if b == 1:
            send_block([(XIN.at[m], bo.at[sec * half + m])], 1, 1)

    def stage4(m, carry):
        stage_e(1, 4, m)
        return carry

    def coef_f(b, stage, m):
        total = take_sums(slot(stage - 1, m))
        VACC[b, 3:4] += total[2:3]
        return norm_backward(b, 0, m, total[0:1], total[1:2])

    def low_f(trio, b, m, coef):
        t2 = zero8
        for q in chunks():
            t2 = add8(t2, back_chunk(trio, b * 2, m, q, HS[b * 2 + 1, m, q : q + CHUNK], coef)[1])
        return t2

    def stage5(m, carry):
        t2 = low_f(low, 1, m, coef_f(1, 5, m))
        r = conv(low, WD.at[2])
        wgrad(2, xc(1, 0, m), low)
        t0, t1 = zero8, zero8
        for q in chunks():
            da = (COT[m, q : q + CHUNK].astype(f32) + part(r, q)).astype(bf16)
            COT[m, q : q + CHUNK] = da
            da = da.astype(f32)
            t0, t1 = add8(t0, da), add8(t1, da * act_of(HS[1, m, q : q + CHUNK]))
        send_sums(slot(5, m), fold_rows(t0), fold_rows(t1), fold_rows(t2))
        send_block([(COT.at[m], eg.at[sec * half + m])], 1, 2)

        @pl.when(m == 1)
        def _():
            to_owners(1, 0)

        return carry

    def buffers(x):
        if x == 0:
            return GS2, GR2, GP2, GO2
        return GS1.at[x - 1], GR1.at[x - 1], GP1.at[x - 1], GO1.at[x - 1]

    def taps(b, x):
        a = ACC.at[b * 2 + (1 if x == 0 else 0)]
        for i in range(3):
            for j in range(3) if x == 0 else (x - 1,):
                out = None
                for t in range(2):
                    for s in range(2):
                        e = 2 * t + s - i
                        if 0 <= e <= 1:
                            r = (2 * t + s) * C
                            c = ((2 - j) * 2 + e) * C
                            d = a[r : r + C, c : c + C]
                            out = d if out is None else out + d
                yield (i * 3 + j if x == 0 else i) * C, out

    def to_pair(b, x):
        gs, gr, _, _ = buffers(x)

        @pl.when(sec != b)
        def _():
            for row, val in taps(b, x):
                gs[row : row + C] = val.astype(bf16)
            to_sibling(gs, gr, gsend.at[x, 0], grecv.at[x, 0])

    def piece(ref, x, p):
        size = GP2.shape[1] if x == 0 else GP1.shape[2]
        return ref.at[pl.ds(pl.multiple_of(p * size, 16), size)]

    def span(ref, x, k):
        size = GP2.shape[1] if x == 0 else GP1.shape[2]
        return ref.at[pl.ds(0, k * size)]

    def owners(x):
        return (GO2.shape[0] // GP2.shape[1]) if x == 0 else (GO1.shape[1] // GP1.shape[2])

    def when_owner(x, p, body):
        if owners(x) == n:
            body()
        else:
            pl.when(p < owners(x))(body)

    def to_owners(b, x):
        gs, gr, gp, _ = buffers(x)

        @pl.when(sec == b)
        def _():
            wait(gr, grecv.at[x, 0])
            for row, val in taps(b, x):
                gs[row : row + C] = (val + gr[row : row + C].astype(f32)).astype(bf16)

            def keep():
                gp[me] = piece(gs, x, me)[...]

            when_owner(x, me, keep)

            def one(d):
                to = lax.rem(me + d, n)

                def go():
                    pltpu.make_async_remote_copy(
                        piece(gs, x, to), gp.at[me], gsend.at[x, 1], grecv.at[x, 1],
                        device_id={"dp": to}, device_id_type=MESH,
                    ).start()

                when_owner(x, to, go)

            every_peer(one)

    def to_all(b, x):
        gs, _, gp, go = buffers(x)
        k = owners(x)

        @pl.when(sec == b)
        def _():
            def mine():
                if n > 1:
                    wait(gp.at[pl.ds(0, n - 1)], grecv.at[x, 1])
                if k > 1:
                    wait(span(gs, x, k - 1), gsend.at[x, 1])
                total = gp[0].astype(f32)
                for d in range(1, n):
                    total = total + gp[d].astype(f32)
                piece(go, x, me)[...] = total.astype(bf16)
                every_peer(
                    lambda d: pltpu.make_async_remote_copy(
                        piece(go, x, me), piece(go, x, me), gsend.at[x, 2], grecv.at[x, 2],
                        device_id=peer(d), device_id_type=MESH,
                    ).start()
                )

            when_owner(x, me, mine)
            if k < n:
                @pl.when(me >= k)
                def _():
                    wait(span(gs, x, k), gsend.at[x, 1])

    def finish(b, x):
        gs, _, gp, go = buffers(x)
        k = owners(x)

        @pl.when(sec == b)
        def _():
            def mine():
                if k > 1:
                    wait(span(go, x, k - 1), grecv.at[x, 2])
                if n > 1:
                    wait(gp.at[pl.ds(0, n - 1)], gsend.at[x, 2])

            when_owner(x, me, mine)
            if k < n:
                @pl.when(me >= k)
                def _():
                    wait(span(go, x, k), grecv.at[x, 2])

        @pl.when(sec != b)
        def _():
            wait(gs, gsend.at[x, 0])

    @pl.when(sec != 0)
    def _():
        wait(WR.at[0, 0], wrsem.at[0])

    prep_forward(0, 0)
    wait(PV.at[0], wrsem.at[2])
    lax.fori_loop(0, half, stage0, 0)

    @pl.when(sec == 0)
    def _():
        wait(WR.at[0, 0], wrsem.at[0])

    wait(WR.at[0, 1], wrsem.at[1])
    for v in range(2):
        wait(WR.at[0, 0], wssem.at[v])
    wait(PV.at[0], wssem.at[2])
    prep_forward(0, 1)
    prep_backward(0, 0)
    lax.fori_loop(0, half, stage1, 0)
    prep_forward(1, 0)
    prep_backward(0, 1)
    lax.fori_loop(0, half, stage2, 0)
    prep_forward(1, 1)
    prep_backward(1, 1)
    lax.fori_loop(0, half, stage3, 0)
    prep_backward(1, 0)
    lax.fori_loop(0, half, stage4, 0)
    to_pair(1, 0)
    lax.fori_loop(0, half, stage5, 0)
    for x in range(1, 4):
        to_pair(1, x)

    def stage6(m, carry):
        stage_e(0, 6, m)

        @pl.when(m == 1)
        def _():
            for x in range(1, 4):
                to_owners(1, x)

        @pl.when(m == 2)
        def _():
            to_all(1, 0)

        return carry

    lax.fori_loop(0, half, stage6, 0)
    finish(1, 0)
    to_pair(0, 0)
    sent_blocks(bo, 0, 0)

    def last_trio(m):
        return xc(1, 1, m), xc(0, 1, m), xc(1, 0, m)

    def stage7(m, carry):
        t2 = low_f(last_trio(m), 0, m, coef_f(0, 7, m))
        wgrad(0, xc(0, 0, m), last_trio(m), (2,))
        send_sums(slot(7, m), fold_rows(t2))

        @pl.when(m == 1)
        def _():
            for x in range(1, 4):
                to_all(1, x)

        @pl.when(m == half - 1)
        def _():
            for x in range(1, 4):
                finish(1, x)

        return carry

    lax.fori_loop(0, half, stage7, 0)
    to_pair(0, 1)

    def stage7b(m, carry):
        wgrad(0, xc(0, 0, m), last_trio(m), (1,))
        return carry

    lax.fori_loop(0, half, stage7b, 0)
    to_pair(0, 2)
    to_owners(0, 0)
    to_owners(0, 1)

    def stage7c(m, carry):
        wgrad(0, xc(0, 0, m), last_trio(m), (0,))
        return carry

    lax.fori_loop(0, half, stage7c, 0)
    to_pair(0, 3)
    to_owners(0, 2)
    sent_blocks(eg, 1, 2)

    def stage8(m, carry):
        r = conv(last_trio(m), WD.at[0])
        for q in chunks():
            da = (COT[m, q : q + CHUNK].astype(f32) + part(r, q)) * inv2
            COT[m, q : q + CHUNK] = da.astype(bf16)
        send_block([(COT.at[m], eg.at[sec * half + m])], 0, 3)

        @pl.when(m == 0)
        def _():
            to_owners(0, 3)

        @pl.when(m == half - 1)
        def _():
            to_all(0, 1)

        return carry

    lax.fori_loop(0, half, stage8, 0)

    for m in range(half):
        VACC[0, 0:1] += take_sums(slot(7, m))[0:1]
    to_sibling(VACC.at[sib], VR, vsem.at[0], vsem.at[1])
    to_all(0, 0)
    to_all(0, 2)
    to_all(0, 3)
    wait(VR, vsem.at[1])
    wait(VR, vsem.at[0])
    gvec[...] = VACC[sec] + VR[...]
    sent_blocks(bo, 1, 1)
    sent_blocks(eg, 0, 3)
    came_blocks(bo, 0, 0)
    came_blocks(bo, 1, 1)
    came_blocks(eg, 1, 2)
    came_blocks(eg, 0, 3)
    for x in (0, 1, 2, 3):
        finish(0, x)


def writer(*refs):
    bo_in, eg_in, go2, go1, gvec, bo, eg, gw1, gw2 = refs[:9]
    vecs, sem = refs[9:15], refs[15]
    copies = []
    for k, (src, dst) in enumerate(((bo_in, bo), (eg_in, eg))):
        for m in range(src.shape[0]):
            for e in range(2):
                copies.append(
                    pltpu.make_async_copy(src.at[m, :, :, pl.ds(e * C, C)], dst.at[m, :, e], sem.at[k, m, e])
                )
                copies[-1].start()
    for k in range(9):
        gw2[k] = go2[k * C : (k + 1) * C].astype(f32)
        gw1[k] = go1[k % 3, k // 3 * C : (k // 3 + 1) * C].astype(f32)
    for k, ref in enumerate(vecs):
        ref[...] = gvec[k : k + 1]
    for copy in copies:
        copy.wait()


def solution(mesh):
    n = mesh.shape["dp"]
    size2, own2 = piece_rows(9 * C, n)
    size1, own1 = piece_rows(3 * C, n)

    def per_device(inputs, channel_mean, channel_std, cotangent, conv_w1, conv_b1, bn_gain1, bn_shift1, conv_w2, conv_b2, bn_gain2, bn_shift2):
        micro, _, H, W, _ = inputs.shape
        half = micro // 2
        Q = H // 2
        field = (micro, Q, 2, W, C)
        pairs = (micro, Q, W, 2 * C)
        anywhere = pl.BlockSpec(memory_space=pl.ANY)
        vmem = pl.BlockSpec(memory_space=pltpu.VMEM)
        D = pltpu.SemaphoreType.DMA
        V = pltpu.VMEM
        mid = pl.pallas_call(
            functools.partial(kernel, n),
            out_shape=[
                V(pairs, bf16),
                V(pairs, bf16),
                V((own2 * size2, C), bf16),
                V((3, own1 * size1, C), bf16),
                V((8, C), f32),
            ],
            in_specs=[anywhere, anywhere, vmem, vmem, anywhere, vmem, vmem, vmem, anywhere, vmem, vmem, vmem],
            out_specs=[vmem] * 5,
            scratch_shapes=[
                V((half, Q, W, 2 * C), bf16),
                V((half, Q, W, 2 * C), bf16),
                V((4 * half + 1, Q + 1, W, 2 * C), bf16),
                V((2, Q + 1, W, 2 * C), bf16),
                V((4, half, Q, W, 2 * C), f32),
                V((4, 3, 2, 2 * C, 2 * C), bf16),
                V((4, 3, 2, 2 * C, 2 * C), bf16),
                V((4, 4 * C, 6 * C), f32),
                V((2, 2, 9, C, C), bf16),
                V((2, 8, C), f32),
                V((4, half, 8, C), f32),
                V((2, 8, C), f32),
                V((8, C), f32),
                V((2 * half, 4, C), f32),
                V((2 * half, n, 4, C), f32),
                V((own2 * size2, C), bf16),
                V((3, own1 * size1, C), bf16),
                V((own2 * size2, C), bf16),
                V((3, own1 * size1, C), bf16),
                V((n, size2, C), bf16),
                V((3, n, size1, C), bf16),
                D((2 * half,)),
                D((2,)),
                D((3,)),
                D((3,)),
                D((2 * half,)),
                D((2 * half,)),
                D((4,)),
                D((4,)),
                D((4,)),
                D((4, 3)),
                D((4, 3)),
                D((2,)),
            ],
            compiler_params=pltpu.CompilerParams(
                collective_id=0, has_side_effects=True, vmem_limit_bytes=VMEM_LIMIT
            ),
        )(
            inputs.reshape(field),
            cotangent.reshape(field),
            channel_mean[None],
            channel_std[None],
            conv_w1.reshape(9, C, C),
            conv_b1,
            bn_gain1,
            bn_shift1,
            conv_w2.reshape(9, C, C),
            conv_b2,
            bn_gain2,
            bn_shift2,
        )
        bo, eg, gw1, gw2, *vecs = pl.pallas_call(
            writer,
            out_shape=[
                jax.ShapeDtypeStruct(field, bf16),
                jax.ShapeDtypeStruct(field, bf16),
                jax.ShapeDtypeStruct((9, C, C), f32),
                jax.ShapeDtypeStruct((9, C, C), f32),
            ]
            + [jax.ShapeDtypeStruct((1, C), f32)] * 6,
            in_specs=[vmem] * 5,
            out_specs=[anywhere, anywhere] + [vmem] * 8,
            scratch_shapes=[D((2, micro, 2))],
        )(*mid)
        whole = (1, micro, 1, H, W, C)
        kernel_shape = (1, 3, 3, C, C)
        return (
            bo.reshape(whole),
            eg.reshape(whole),
            gw1.reshape(kernel_shape),
            vecs[0],
            vecs[1],
            vecs[2],
            gw2.reshape(kernel_shape),
            vecs[3],
            vecs[4],
            vecs[5],
        )

    in_specs = (
        P(None, "dp", None, None, None),
        P(),
        P(),
        P(None, "dp", None, None, None),
        P("section", None, None, None, None),
        P("section", None),
        P("section", None),
        P("section", None),
        P("section", None, None, None, None),
        P("section", None),
        P("section", None),
        P("section", None),
    )
    out_specs = (
        P("section", None, "dp", None, None, None),
        P("section", None, "dp", None, None, None),
        P("section", None, None, None, None),
        P("section", None),
        P("section", None),
        P("section", None),
        P("section", None, None, None, None),
        P("section", None),
        P("section", None),
        P("section", None),
    )
    return jax.shard_map(per_device, mesh=mesh, in_specs=in_specs, out_specs=out_specs, check_vma=False)
```

time: 134 us -> 116 us (0.87)
  Pallas kernels: 123 us -> 109 us
  local copies, waits for them, and re-layouts: 10.5 us -> 5.96 us
    pallas_call x1 -> x2, Pallas kernels: 123 us -> 109 us  [the longest x1 101 us: per_device(): pl.pallas_call(functools.partial(kernel, n), out_shape=[V(pairs, bf16), V...]
    unnamed x10, local copies, waits for them, and re-layouts: 9.07 us -> 5.96 us
    slice x1 -> x0, local copies, waits for them, and re-layouts: 1.44 us -> none  [per_device(): gvec[5:6]]
where the time goes in v2:
time: 116 us; the launch traced here: 115 us
  Pallas kernels  109 us (94%)
  local copies, waits for them, and re-layouts  5.96 us (5%)
    pallas_call x1, Pallas kernels, per_device(): pl.pallas_call(functools.partial(kernel, n), out_shape=[V(pairs, bf16), V...  101 us
    pallas_call x1, Pallas kernels, per_device(): pl.pallas_call(writer, out_shape=[jax.ShapeDtypeStruct(field, bf16), jax....  8.12 us
    unnamed x10, local copies, waits for them, and re-layouts  5.96 us

profile of v2, /device:TPU:0, one launch (start us, length us, event | category | flops | bytes accessed | tf_op | source)
XLA Modules:
  0.0 115.5 jit_solution(14727456302806084643)
XLA Ops:
  0.6 100.6 %shard_map.195 = (bf16[8,16,64,256]{3,2,1,0:T(8,128)(2,1)S(1)}, bf16[8,16,64,256]{3,2,1,0:T(8,128)(2,1)S(1)}, bf16[1200,128]{1,0:T(8,128)(2,1)S(1)}, bf16[3,384,128]{2,1,0:T(8,128)(2,1)S(1)}, f32[8,128]{1,0:T(8,128)S(1)}) custom-call(bf16[8,16,2,64,128]{4,3,2,1,0:T(8,128)(2,1)} %bitcast.14, bf16[8,16,2,64,128]{4,3,2,1,0:T(8,128)(2,1)} %bitcast.15, ...), custom_call_target="tpu_custom_call" | custom-call | tf_op jit(solution)/shard_map/pallas_call | solution.py:681
  101.2 0.0 copy-start
  101.2 1.9 %copy-done = bf16[8,16,64,256]{3,2,1,0:T(8,128)(2,1)} copy-done((bf16[8,16,64,256]{3,2,1,0:T(8,128)(2,1)}, bf16[8,16,64,256]{3,2,1,0:T(8,128)(2,1)S(1)}, u32[]{:S(2)}) %copy-start) | copy-done | bytes 4194328
  103.2 0.0 copy-start.1
  103.2 2.0 %copy-done.1 = bf16[8,16,64,256]{3,2,1,0:T(8,128)(2,1)} copy-done((bf16[8,16,64,256]{3,2,1,0:T(8,128)(2,1)}, bf16[8,16,64,256]{3,2,1,0:T(8,128)(2,1)S(1)}, u32[]{:S(2)}) %copy-start.1) | copy-done | bytes 4194328
  105.1 0.0 copy-start.2
  105.2 0.7 copy-done.2
  105.9 0.0 copy-start.3
  105.9 0.7 copy-done.3
  106.6 0.0 copy-start.4
  106.6 0.6 copy-done.4
  107.2 8.1 %shard_map.196 = (bf16[8,16,2,64,128]{4,3,2,1,0:T(8,128)(2,1)}, bf16[8,16,2,64,128]{4,3,2,1,0:T(8,128)(2,1)}, f32[9,128,128]{2,1,0:T(8,128)}, f32[9,128,128]{2,1...) custom-call(bf16[8,16,64,256]{3,2,1,0:T(8,128)(2,1)} %copy-done, ...), custom_call_target="tpu_custom_call" | custom-call | tf_op jit(solution)/shard_map/pallas_call | solution.py:744
Async XLA Ops:
  101.2 1.9 %copy-start = (bf16[8,16,64,256]{3,2,1,0:T(8,128)(2,1)}, bf16[8,16,64,256]{3,2,1,0:T(8,128)(2,1)S(1)}, u32[]{:S(2)}) copy-start(bf16[8,16,64,256]{3,2,1,0:T(8,128)(2,1)S(1)} %get-tuple-element.25.refs_0_) | copy-start | bytes 12582916
  103.2 2.0 %copy-start.1 = (bf16[8,16,64,256]{3,2,1,0:T(8,128)(2,1)}, bf16[8,16,64,256]{3,2,1,0:T(8,128)(2,1)S(1)}, u32[]{:S(2)}) copy-start(bf16[8,16,64,256]{3,2,1,0:T(8,128)(2,1)S(1)} %get-tuple-element.26.refs_1_) | copy-start | bytes 12582916
  105.1 0.7 copy-start.2
  105.9 0.7 copy-start.3
  106.6 0.6 copy-start.4

commit v3 on v2

--- a/solution.py
+++ b/solution.py
@@ -12,25 +12,19 @@
 bf16 = jnp.bfloat16
 f32 = jnp.float32
 C = 128
-CHUNK = 2
-VMEM_LIMIT = 52 * 2**20
+VMEM_LIMIT = 55 * 2**20
 
 
 def dot(a, b):
     return jnp.dot(a, b, preferred_element_type=f32)
 
 
-def twice(v):
-    return jnp.concatenate([v, v], axis=-1)
-
-
 def fold_rows(v):
-    one = jnp.sum(v, axis=0, keepdims=True)
-    return one[:, :C] + one[:, C:]
+    return jnp.sum(v, axis=0, keepdims=True)
 
 
 def piece_rows(rows, n):
-    size = -(-rows // n // 16) * 16
+    size = -(-rows // max(1, n // 2) // 16) * 16
     return size, -(-rows // size)
 
 
@@ -38,8 +32,8 @@
     (
         inp, cot, mean, std, w1, b1, g1, s1, w2, b2, g2, s2,
         bo, eg, GO2, GO1, gvec,
-        XIN, COT, XC, LB, HS, WF, WD, ACC, WR, PV, ST, VACC, VR,
-        MSG, SLOT, GS2, GS1, GR2, GR1, GP2, GP1,
+        XIN, COT, XC, LOW0, LOW1, HS, WF, WD, ACC, WR, PV, ST, VACC, VR,
+        MSG, SLOT, PS2, PS1, GS2, GS1, GR2, GR1, GP2, GP1,
         isem, wlsem, wssem, wrsem, msend, mrecv, olsem, ossem, orsem, gsend, grecv, vsem,
     ) = refs
     micro = inp.shape[0]
@@ -88,16 +82,17 @@
         PV[sec, v : v + 1] = ref[...]
 
     halo = jnp.zeros((W, C), bf16)
-    for j in range(2):
-        LB[j, 0, :, 0:C] = halo
-        LB[j, Q, :, C : 2 * C] = halo
+    for j in range(3):
+        LOW0[j, 0, :, 0:C] = halo
+        LOW0[j, Q, :, C : 2 * C] = halo
+    LOW1[...] = jnp.zeros(LOW1.shape, bf16)
 
     def zero_halo(i, carry):
         XC[i, 0, :, 0:C] = halo
         XC[i, Q, :, C : 2 * C] = halo
         return carry
 
-    lax.fori_loop(0, 4 * half + 1, zero_halo, 0)
+    lax.fori_loop(0, 4 * half, zero_halo, 0)
     empty = jnp.zeros((C, C), bf16)
     for i in range(4):
         ACC[i] = jnp.zeros(ACC.shape[1:], f32)
@@ -106,8 +101,8 @@
                 ref[i, j, 0, 0:C, C : 2 * C] = empty
                 ref[i, j, 1, C : 2 * C, 0:C] = empty
     VACC[...] = jnp.zeros(VACC.shape, f32)
-    GS2[...] = jnp.zeros(GS2.shape, bf16)
-    GS1[...] = jnp.zeros(GS1.shape, bf16)
+    for ref in (PS2, PS1, GS2, GS1):
+        ref[...] = jnp.zeros(ref.shape, bf16)
 
     pl.semaphore_wait(barrier, n)
 
@@ -165,7 +160,7 @@
         ST[b * 2 + v, m, 0:1] = mu
         ST[b * 2 + v, m, 1:2] = rstd
         sc = vec(b, 1 + 3 * v) * rstd
-        return twice(sc), twice(vec(b, 2 + 3 * v) - mu * sc)
+        return sc, vec(b, 2 + 3 * v) - mu * sc
 
     def norm_backward(b, v, m, shift_sum, prod_sum):
         mu = ST[b * 2 + v, m, 0:1]
@@ -176,17 +171,18 @@
         ca = vec(b, 1 + 3 * v) * rstd
         cc = -ca * rstd * gain_sum / count
         cb = -ca * shift_sum / count - cc * mu
-        return twice(ca), twice(cb), twice(cc)
-
-    def put(trio, q, v):
-        k = v.shape[0]
+        return ca, cb, cc
+
+    def spot(q, e):
+        return q + e, slice(None), slice((1 - e) * C, (2 - e) * C)
+
+    def put(trio, q, e, v):
         for j, ref in enumerate(trio):
-            u = (v if j == 1 else pltpu.roll(v, 1 if j == 0 else W - 1, 1)).astype(bf16)
-            ref[q : q + k, :, C : 2 * C] = u[:, :, :C]
-            ref[q + 1 : q + k + 1, :, 0:C] = u[:, :, C:]
-
-    def get(center, q, k):
-        return jnp.concatenate([center[q : q + k, :, C : 2 * C], center[q + 1 : q + k + 1, :, 0:C]], axis=-1)
+            ref[spot(q, e)] = (v if j == 1 else pltpu.roll(v, 1 if j == 0 else W - 1, 0)).astype(bf16)
+
+    def get_all(center):
+        both = [center[0:Q, :, C : 2 * C], center[1 : Q + 1, :, 0:C]]
+        return jnp.concatenate(both, axis=-1).reshape(rows, 2 * C)
 
     def conv(trio, w):
         acc = None
@@ -199,41 +195,42 @@
     def wgrad(i, center, trio, which=(0, 1, 2)):
         left = jnp.concatenate([center[0:Q].reshape(rows, 2 * C), center[1 : Q + 1].reshape(rows, 2 * C)], axis=-1)
         for j in which:
-            right = get(trio[j], 0, Q).reshape(rows, 2 * C)
             ACC[i, :, j * 2 * C : (j + 1) * 2 * C] += lax.dot_general(
-                left, right, (((0,), (0,)), ((), ())), preferred_element_type=f32
+                left, get_all(trio[j]), (((0,), (0,)), ((), ())), preferred_element_type=f32
             )
 
-    def chunks():
-        return range(0, Q, CHUNK)
-
-    def part(r, q):
-        return r[q * W : (q + CHUNK) * W].reshape(CHUNK, W, 2 * C)
+    def planes():
+        for q in range(Q):
+            for e in range(2):
+                yield q, e, (q, slice(None), slice(e * C, e * C + C))
+
+    def part(r, q, e):
+        return r[q * W : (q + 1) * W, e * C : (e + 1) * C]
 
     def add8(total, v):
-        return total + jnp.sum(v.reshape(-1, 8, 2 * C), axis=0)
-
-    zero8 = jnp.zeros((8, 2 * C), f32)
+        return total + jnp.sum(v.reshape(-1, 8, C), axis=0)
+
+    zero8 = jnp.zeros((8, C), f32)
 
     def act_of(h):
         return h + h * jnp.tanh(h)
 
-    mean2 = twice(mean[...])
-    inv2 = twice(1.0 / std[...])
-
-    def standard(m, q):
-        return (XIN[m, q : q + CHUNK].astype(f32) - mean2) * inv2
+    mean1 = mean[...]
+    inv1 = 1.0 / std[...]
+
+    def standard(m, at):
+        return (XIN[(m, *at)].astype(f32) - mean1) * inv1
 
     def after_conv(b, v, m, r, cots):
-        bias = twice(vec(b, 3 * v) * 0.5)
+        bias = vec(b, 3 * v) * 0.5
         t0, t1, t2, t3 = zero8, zero8, zero8, zero8
-        for q in chunks():
-            h = part(r, q) + bias
-            HS[b * 2 + v, m, q : q + CHUNK] = h
+        for q, e, at in planes():
+            h = part(r, q, e) + bias
+            HS[(b * 2 + v, m, *at)] = h
             act = act_of(h)
             t0, t1 = add8(t0, act), add8(t1, act * act)
             if cots:
-                dy = COT[m, q : q + CHUNK].astype(f32)
+                dy = COT[(m, *at)].astype(f32)
                 t2, t3 = add8(t2, dy), add8(t3, dy * act)
         sums = (fold_rows(t0), fold_rows(t1))
         if cots:
@@ -271,9 +268,10 @@
         return XC.at[(b * 2 + v) * half + m]
 
     def trio_of(center):
-        return LB.at[0], center, LB.at[1]
-
-    low = trio_of(XC.at[4 * half])
+        return LOW0.at[0], center, LOW0.at[2]
+
+    low0 = tuple(LOW0.at[j] for j in range(3))
+    low1 = tuple(LOW1.at[j] for j in range(3))
 
     def slot(stage, m):
         return (stage % 2) * half + m
@@ -281,8 +279,8 @@
     def stage0(m, carry):
         wait(XIN.at[m], isem.at[m])
         trio = trio_of(xc(0, 0, m))
-        for q in chunks():
-            put(trio, q, standard(m, q))
+        for q, e, at in planes():
+            put(trio, q, e, standard(m, at))
         send_sums(slot(0, m), *after_conv(0, 0, m, conv(trio, WF.at[0]), False))
         return carry
 
@@ -291,8 +289,8 @@
         if b == 1:
             wait(COT.at[m], isem.at[half + m])
         trio = trio_of(xc(b, 1, m))
-        for q in chunks():
-            put(trio, q, act_of(HS[b * 2, m, q : q + CHUNK]) * sc + sh)
+        for q, e, at in planes():
+            put(trio, q, e, act_of(HS[(b * 2, m, *at)]) * sc + sh)
         send_sums(slot(stage, m), *after_conv(b, 1, m, conv(trio, WF.at[b * 2 + 1]), b == 1))
 
     def stage1(m, carry):
@@ -303,8 +301,8 @@
         sc, sh = norm_forward(0, 1, m, take_sums(slot(1, m)))
         center = xc(1, 0, m)
         trio = trio_of(center)
-        for q in chunks():
-            put(trio, q, standard(m, q) + (act_of(HS[1, m, q : q + CHUNK]) * sc + sh))
+        for q, e, at in planes():
+            put(trio, q, e, standard(m, at) + (act_of(HS[(1, m, *at)]) * sc + sh))
         send_sums(slot(2, m), *after_conv(1, 0, m, conv(trio, WF.at[2]), False))
         send_block(
             [
@@ -320,16 +318,16 @@
         stage_norm1(1, 3, m)
         return carry
 
-    def back_chunk(trio, i, m, q, dy, coef):
+    def back_plane(trio, i, m, q, e, at, dy, coef):
         ca, cb, cc = coef
-        h = HS[i, m, q : q + CHUNK]
+        h = HS[(i, m, *at)]
         u = 1.0 + jnp.tanh(h)
         act = h * u
         dp = (ca * dy + (cc * act + cb)) * (act + (0.5 * u) * (1.0 - act))
-        put(trio, q, dp)
+        put(trio, q, e, dp)
         return act, dp
 
-    def stage_e(b, stage, m):
+    def step_e(b, stage, m, trio, before):
         total = take_sums(slot(stage - 1, m))
         if b == 1:
             sc, sh = norm_forward(1, 1, m, total)
@@ -339,26 +337,21 @@
             VACC[1, 0:1] += total[2:3]
         t0, t1, t2 = zero8, zero8, zero8
         i = b * 2 + 1
-        for q in chunks():
-            dy = COT[m, q : q + CHUNK].astype(f32)
-            act, dp = back_chunk(low, i, m, q, dy, coef)
+        wgrad(*before)
+        for q, e, at in planes():
+            act, dp = back_plane(trio, i, m, q, e, at, COT[(m, *at)].astype(f32), coef)
             t2 = add8(t2, dp)
             if b == 1:
-                final = get(xc(1, 0, m), q, CHUNK).astype(f32) + (act * sc + sh)
-                XIN[m, q : q + CHUNK] = final.astype(bf16)
-        r = conv(low, WD.at[i])
-        wgrad(i, xc(b, 1, m), low)
-        for q in chunks():
-            dn = part(r, q)
-            HS[i, m, q : q + CHUNK] = dn
-            t0, t1 = add8(t0, dn), add8(t1, dn * act_of(HS[b * 2, m, q : q + CHUNK]))
+                final = xc(1, 0, m)[spot(q, e)].astype(f32) + (act * sc + sh)
+                XIN[(m, *at)] = final.astype(bf16)
+        r = conv(trio, WD.at[i])
+        for q, e, at in planes():
+            dn = part(r, q, e)
+            HS[(i, m, *at)] = dn
+            t0, t1 = add8(t0, dn), add8(t1, dn * act_of(HS[(b * 2, m, *at)]))
         send_sums(slot(stage, m), fold_rows(t0), fold_rows(t1), fold_rows(t2))
         if b == 1:
             send_block([(XIN.at[m], bo.at[sec * half + m])], 1, 1)
-
-    def stage4(m, carry):
-        stage_e(1, 4, m)
-        return carry
 
     def coef_f(b, stage, m):
         total = take_sums(slot(stage - 1, m))
@@ -367,33 +360,42 @@
 
     def low_f(trio, b, m, coef):
         t2 = zero8
-        for q in chunks():
-            t2 = add8(t2, back_chunk(trio, b * 2, m, q, HS[b * 2 + 1, m, q : q + CHUNK], coef)[1])
+        for q, e, at in planes():
+            t2 = add8(t2, back_plane(trio, b * 2, m, q, e, at, HS[(b * 2 + 1, m, *at)], coef)[1])
         return t2
 
-    def stage5(m, carry):
-        t2 = low_f(low, 1, m, coef_f(1, 5, m))
-        r = conv(low, WD.at[2])
-        wgrad(2, xc(1, 0, m), low)
+    def step_f(b, stage, m, trio, before):
+        coef = coef_f(1, stage, m)
+        wgrad(*before)
+        t2 = low_f(trio, 1, m, coef)
+        r = conv(trio, WD.at[2])
         t0, t1 = zero8, zero8
-        for q in chunks():
-            da = (COT[m, q : q + CHUNK].astype(f32) + part(r, q)).astype(bf16)
-            COT[m, q : q + CHUNK] = da
+        for q, e, at in planes():
+            da = (COT[(m, *at)].astype(f32) + part(r, q, e)).astype(bf16)
+            COT[(m, *at)] = da
             da = da.astype(f32)
-            t0, t1 = add8(t0, da), add8(t1, da * act_of(HS[1, m, q : q + CHUNK]))
-        send_sums(slot(5, m), fold_rows(t0), fold_rows(t1), fold_rows(t2))
+            t0, t1 = add8(t0, da), add8(t1, da * act_of(HS[(1, m, *at)]))
+        send_sums(slot(stage, m), fold_rows(t0), fold_rows(t1), fold_rows(t2))
         send_block([(COT.at[m], eg.at[sec * half + m])], 1, 2)
 
-        @pl.when(m == 1)
-        def _():
-            to_owners(1, 0)
-
-        return carry
+    def back_stage(step, b, stage, own, last, after):
+        def pair(k, carry):
+            m = 2 * k
+            first = lax.div(1, k + 1)
+            i = own + (last - own) * first
+            x = own * half + m - 1 + ((last - own) * half + half) * first
+            step(b, stage, m, low0, (i, XC.at[x], low1))
+            step(b, stage, m + 1, low1, (own, xc(own // 2, own % 2, m), low0))
+            for at, body in after:
+                pl.when(k == at)(body)
+            return carry
+
+        lax.fori_loop(0, half // 2, pair, 0)
 
     def buffers(x):
         if x == 0:
-            return GS2, GR2, GP2, GO2
-        return GS1.at[x - 1], GR1.at[x - 1], GP1.at[x - 1], GO1.at[x - 1]
+            return PS2, GS2, GR2, GP2, GO2
+        return PS1.at[x - 1], GS1.at[x - 1], GR1.at[x - 1], GP1.at[x - 1], GO1.at[x - 1]
 
     def taps(b, x):
         a = ACC.at[b * 2 + (1 if x == 0 else 0)]
@@ -411,107 +413,94 @@
                 yield (i * 3 + j if x == 0 else i) * C, out
 
     def to_pair(b, x):
-        gs, gr, _, _ = buffers(x)
+        ps, _, gr, _, _ = buffers(x)
 
         @pl.when(sec != b)
         def _():
             for row, val in taps(b, x):
-                gs[row : row + C] = val.astype(bf16)
-            to_sibling(gs, gr, gsend.at[x, 0], grecv.at[x, 0])
+                ps[row : row + C] = val.astype(bf16)
+            to_sibling(ps, gr, gsend.at[x, 0], grecv.at[x, 0])
+
+    def piece_size(x):
+        return GP2.shape[1] if x == 0 else GP1.shape[2]
+
+    def owners(x):
+        k = (GO2.shape[0] if x == 0 else GO1.shape[1]) // piece_size(x)
+        return k, (n - k) // 2
 
     def piece(ref, x, p):
-        size = GP2.shape[1] if x == 0 else GP1.shape[2]
+        size = piece_size(x)
         return ref.at[pl.ds(pl.multiple_of(p * size, 16), size)]
 
     def span(ref, x, k):
-        size = GP2.shape[1] if x == 0 else GP1.shape[2]
-        return ref.at[pl.ds(0, k * size)]
-
-    def owners(x):
-        return (GO2.shape[0] // GP2.shape[1]) if x == 0 else (GO1.shape[1] // GP1.shape[2])
-
-    def when_owner(x, p, body):
-        if owners(x) == n:
-            body()
-        else:
-            pl.when(p < owners(x))(body)
+        return ref.at[pl.ds(0, k * piece_size(x))]
 
     def to_owners(b, x):
-        gs, gr, gp, _ = buffers(x)
+        _, gs, gr, gp, _ = buffers(x)
+        k, first = owners(x)
 
         @pl.when(sec == b)
         def _():
             wait(gr, grecv.at[x, 0])
             for row, val in taps(b, x):
                 gs[row : row + C] = (val + gr[row : row + C].astype(f32)).astype(bf16)
-
-            def keep():
-                gp[me] = piece(gs, x, me)[...]
-
-            when_owner(x, me, keep)
-
-            def one(d):
-                to = lax.rem(me + d, n)
-
-                def go():
+            for d in range(k):
+                p = lax.rem(me + d, k)
+
+                @pl.when(first + p == me)
+                def _():
+                    gp[me] = piece(gs, x, p)[...]
+
+                @pl.when(first + p != me)
+                def _():
                     pltpu.make_async_remote_copy(
-                        piece(gs, x, to), gp.at[me], gsend.at[x, 1], grecv.at[x, 1],
-                        device_id={"dp": to}, device_id_type=MESH,
+                        piece(gs, x, p), gp.at[me], gsend.at[x, 1], grecv.at[x, 1],
+                        device_id={"dp": first + p}, device_id_type=MESH,
                     ).start()
 
-                when_owner(x, to, go)
-
-            every_peer(one)
+    def when_owner(b, x, mine, other):
+        k, first = owners(x)
+        own = (me >= first) & (me < first + k)
+        pl.when((sec == b) & own)(mine)
+        pl.when((sec == b) & jnp.logical_not(own))(other)
 
     def to_all(b, x):
-        gs, _, gp, go = buffers(x)
-        k = owners(x)
-
-        @pl.when(sec == b)
-        def _():
-            def mine():
-                if n > 1:
-                    wait(gp.at[pl.ds(0, n - 1)], grecv.at[x, 1])
-                if k > 1:
-                    wait(span(gs, x, k - 1), gsend.at[x, 1])
-                total = gp[0].astype(f32)
-                for d in range(1, n):
-                    total = total + gp[d].astype(f32)
-                piece(go, x, me)[...] = total.astype(bf16)
-                every_peer(
-                    lambda d: pltpu.make_async_remote_copy(
-                        piece(go, x, me), piece(go, x, me), gsend.at[x, 2], grecv.at[x, 2],
-                        device_id=peer(d), device_id_type=MESH,
-                    ).start()
-                )
-
-            when_owner(x, me, mine)
-            if k < n:
-                @pl.when(me >= k)
-                def _():
-                    wait(span(gs, x, k), gsend.at[x, 1])
+        _, gs, _, gp, go = buffers(x)
+        k, first = owners(x)
+
+        def mine():
+            if n > 1:
+                wait(gp.at[pl.ds(0, n - 1)], grecv.at[x, 1])
+            if k > 1:
+                wait(span(gs, x, k - 1), gsend.at[x, 1])
+            total = gp[0].astype(f32)
+            for d in range(1, n):
+                total = total + gp[d].astype(f32)
+            at = piece(go, x, me - first)
+            at[...] = total.astype(bf16)
+            every_peer(
+                lambda d: pltpu.make_async_remote_copy(
+                    at, at, gsend.at[x, 2], grecv.at[x, 2], device_id=peer(d), device_id_type=MESH
+                ).start()
+            )
+
+        when_owner(b, x, mine, lambda: wait(span(gs, x, k), gsend.at[x, 1]))
 
     def finish(b, x):
-        gs, _, gp, go = buffers(x)
-        k = owners(x)
-
-        @pl.when(sec == b)
-        def _():
-            def mine():
-                if k > 1:
-                    wait(span(go, x, k - 1), grecv.at[x, 2])
-                if n > 1:
-                    wait(gp.at[pl.ds(0, n - 1)], gsend.at[x, 2])
-
-            when_owner(x, me, mine)
-            if k < n:
-                @pl.when(me >= k)
-                def _():
-                    wait(span(go, x, k), grecv.at[x, 2])
+        ps, _, _, gp, go = buffers(x)
+        k, _ = owners(x)
+
+        def mine():
+            if k > 1:
+                wait(span(go, x, k - 1), grecv.at[x, 2])
+            if n > 1:
+                wait(gp.at[pl.ds(0, n - 1)], gsend.at[x, 2])
+
+        when_owner(b, x, mine, lambda: wait(span(go, x, k), grecv.at[x, 2]))
 
         @pl.when(sec != b)
         def _():
-            wait(gs, gsend.at[x, 0])
+            wait(ps, gsend.at[x, 0])
 
     @pl.when(sec != 0)
     def _():
@@ -539,86 +528,68 @@
     prep_backward(1, 1)
     lax.fori_loop(0, half, stage3, 0)
     prep_backward(1, 0)
-    lax.fori_loop(0, half, stage4, 0)
-    to_pair(1, 0)
-    lax.fori_loop(0, half, stage5, 0)
-    for x in range(1, 4):
-        to_pair(1, x)
-
-    def stage6(m, carry):
-        stage_e(0, 6, m)
-
-        @pl.when(m == 1)
-        def _():
-            for x in range(1, 4):
-                to_owners(1, x)
-
-        @pl.when(m == 2)
-        def _():
-            to_all(1, 0)
-
-        return carry
-
-    lax.fori_loop(0, half, stage6, 0)
-    finish(1, 0)
-    to_pair(0, 0)
+    w1_parts = (1, 2, 3)
+    back_stage(step_e, 1, 4, 3, 3, [])
+    back_stage(
+        step_f, 1, 5, 2, 3, [(0, lambda: to_pair(1, 0)), (half // 2 - 1, lambda: to_owners(1, 0))]
+    )
+    back_stage(
+        step_e,
+        0,
+        6,
+        1,
+        2,
+        [
+            (0, lambda: [to_pair(1, x) for x in w1_parts] and None),
+            (half // 2 - 1, lambda: [to_owners(1, x) for x in w1_parts] and to_all(1, 0)),
+        ],
+    )
     sent_blocks(bo, 0, 0)
 
     def last_trio(m):
         return xc(1, 1, m), xc(0, 1, m), xc(1, 0, m)
 
-    def stage7(m, carry):
-        t2 = low_f(last_trio(m), 0, m, coef_f(0, 7, m))
-        wgrad(0, xc(0, 0, m), last_trio(m), (2,))
-        send_sums(slot(7, m), fold_rows(t2))
-
-        @pl.when(m == 1)
-        def _():
-            for x in range(1, 4):
-                to_all(1, x)
-
-        @pl.when(m == half - 1)
-        def _():
-            for x in range(1, 4):
-                finish(1, x)
-
-        return carry
-
-    lax.fori_loop(0, half, stage7, 0)
+    for m in range(half):
+        coef = coef_f(0, 7, m)
+        if m == 0:
+            wgrad(1, xc(0, 1, half - 1), low1)
+        else:
+            wgrad(0, xc(0, 0, m - 1), last_trio(m - 1), (2, 1))
+        send_sums(slot(7, m), fold_rows(low_f(last_trio(m), 0, m, coef)))
+        if m == 0:
+            to_pair(0, 0)
+        if m == 2:
+            to_owners(0, 0)
+    wgrad(0, xc(0, 0, half - 1), last_trio(half - 1), (2, 1))
     to_pair(0, 1)
-
-    def stage7b(m, carry):
-        wgrad(0, xc(0, 0, m), last_trio(m), (1,))
-        return carry
-
-    lax.fori_loop(0, half, stage7b, 0)
     to_pair(0, 2)
-    to_owners(0, 0)
-    to_owners(0, 1)
-
-    def stage7c(m, carry):
+
+    def last_column(m, carry):
         wgrad(0, xc(0, 0, m), last_trio(m), (0,))
         return carry
 
-    lax.fori_loop(0, half, stage7c, 0)
+    lax.fori_loop(0, half, last_column, 0)
     to_pair(0, 3)
+    to_owners(0, 1)
     to_owners(0, 2)
+    for x in w1_parts:
+        to_all(1, x)
     sent_blocks(eg, 1, 2)
 
     def stage8(m, carry):
         r = conv(last_trio(m), WD.at[0])
-        for q in chunks():
-            da = (COT[m, q : q + CHUNK].astype(f32) + part(r, q)) * inv2
-            COT[m, q : q + CHUNK] = da.astype(bf16)
+        for q, e, at in planes():
+            da = (COT[(m, *at)].astype(f32) + part(r, q, e)) * inv1
+            COT[(m, *at)] = da.astype(bf16)
         send_block([(COT.at[m], eg.at[sec * half + m])], 0, 3)
 
         @pl.when(m == 0)
         def _():
             to_owners(0, 3)
 
-        @pl.when(m == half - 1)
-        def _():
-            to_all(0, 1)
+        @pl.when(m == 2)
+        def _():
+            to_all(0, 0)
 
         return carry
 
@@ -627,9 +598,8 @@
     for m in range(half):
         VACC[0, 0:1] += take_sums(slot(7, m))[0:1]
     to_sibling(VACC.at[sib], VR, vsem.at[0], vsem.at[1])
-    to_all(0, 0)
-    to_all(0, 2)
-    to_all(0, 3)
+    for x in w1_parts:
+        to_all(0, x)
     wait(VR, vsem.at[1])
     wait(VR, vsem.at[0])
     gvec[...] = VACC[sec] + VR[...]
@@ -639,8 +609,9 @@
     came_blocks(bo, 1, 1)
     came_blocks(eg, 1, 2)
     came_blocks(eg, 0, 3)
-    for x in (0, 1, 2, 3):
-        finish(0, x)
+    for b in (1, 0):
+        for x in range(4):
+            finish(b, x)
 
 
 def writer(*refs):
@@ -692,8 +663,9 @@
             scratch_shapes=[
                 V((half, Q, W, 2 * C), bf16),
                 V((half, Q, W, 2 * C), bf16),
-                V((4 * half + 1, Q + 1, W, 2 * C), bf16),
-                V((2, Q + 1, W, 2 * C), bf16),
+                V((4 * half, Q + 1, W, 2 * C), bf16),
+                V((3, Q + 1, W, 2 * C), bf16),
+                V((3, Q + 1, W, 2 * C), bf16),
                 V((4, half, Q, W, 2 * C), f32),
                 V((4, 3, 2, 2 * C, 2 * C), bf16),
                 V((4, 3, 2, 2 * C, 2 * C), bf16),
@@ -705,6 +677,8 @@
                 V((8, C), f32),
                 V((2 * half, 4, C), f32),
                 V((2 * half, n, 4, C), f32),
+                V((own2 * size2, C), bf16),
+                V((3, own1 * size1, C), bf16),
                 V((own2 * size2, C), bf16),
                 V((3, own1 * size1, C), bf16),
                 V((own2 * size2, C), bf16),
@@ -753,7 +727,8 @@
             in_specs=[vmem] * 5,
             out_specs=[anywhere, anywhere] + [vmem] * 8,
             scratch_shapes=[D((2, micro, 2))],
-        )(*mid)
+            compiler_params=pltpu.CompilerParams(vmem_limit_bytes=8 * 2**20),
+        )(*[pltpu.with_memory_space_constraint(v, pltpu.VMEM) for v in mid])
         whole = (1, micro, 1, H, W, C)
         kernel_shape = (1, 3, 3, C, C)
         return (

time: 116 us -> 97.4 us (0.84)
  Pallas kernels: 109 us -> 96.4 us
  local copies, waits for them, and re-layouts: 5.96 us -> 0 us
    pallas_call x1, Pallas kernels: 101 us -> 91.9 us  [per_device(): pl.pallas_call(functools.partial(kernel, n), out_shape=[V(pairs, bf16), V...]
    unnamed x10 -> x0, local copies, waits for them, and re-layouts: 5.96 us -> none
    pallas_call x1, Pallas kernels: 8.12 us -> 4.57 us  [per_device(): pl.pallas_call(writer, out_shape=[jax.ShapeDtypeStruct(field, bf16), jax....]
where the time goes in v3:
time: 97.4 us; the launch traced here: 97.3 us
  Pallas kernels  96.4 us (99%)
    pallas_call x1, Pallas kernels, per_device(): pl.pallas_call(functools.partial(kernel, n), out_shape=[V(pairs, bf16), V...  91.9 us
    pallas_call x1, Pallas kernels, per_device(): pl.pallas_call(writer, out_shape=[jax.ShapeDtypeStruct(field, bf16), jax....  4.57 us

profile of v3, /device:TPU:0, one launch (start us, length us, event | category | flops | bytes accessed | tf_op | source)
XLA Modules:
  0.0 97.3 jit_solution(6594198804082757151)
XLA Ops:
  0.6 91.9 %shard_map.195 = (bf16[8,16,64,256]{3,2,1,0:T(8,128)(2,1)S(1)}, bf16[8,16,64,256]{3,2,1,0:T(8,128)(2,1)S(1)}, bf16[1152,128]{1,0:T(8,128)(2,1)S(1)}, bf16[3,384,128]{2,1,0:T(8,128)(2,1)S(1)}, f32[8,128]{1,0:T(8,128)S(1)}) custom-call(bf16[8,16,2,64,128]{4,3,2,1,0:T(8,128)(2,1)} %bitcast.14, bf16[8,16,2,64,128]{4,3,2,1,0:T(8,128)(2,1)} %bitcast.15, ...), custom_call_target="tpu_custom_call" | custom-call | tf_op jit(solution)/shard_map/pallas_call | solution.py:652
  92.5 4.6 %shard_map.196 = (bf16[8,16,2,64,128]{4,3,2,1,0:T(8,128)(2,1)}, bf16[8,16,2,64,128]{4,3,2,1,0:T(8,128)(2,1)}, f32[9,128,128]{2,1,0:T(8,128)}, f32[9,128,128]{2,1...) custom-call(bf16[8,16,64,256]{3,2,1,0:T(8,128)(2,1)S(1)} %get-tuple-, ...), custom_call_target="tpu_custom_call" | custom-call | tf_op jit(solution)/shard_map/pallas_call | solution.py:718

commit v4 on v3

--- a/solution.py
+++ b/solution.py
@@ -23,17 +23,31 @@
     return jnp.sum(v, axis=0, keepdims=True)
 
 
+PARTS = ((1, (0, 1, 2)), (0, (0, 1)), (0, (2,)))
+
+
+def part_rows(x):
+    return 3 * len(PARTS[x][1]) * C
+
+
+def plane_of(n):
+    plane = min(d for d in range(1, n + 1) if n % d == 0 and d * d >= n)
+    planes = n // plane
+    return plane, planes, min(2, max(1, planes // 2))
+
+
 def piece_rows(rows, n):
-    size = -(-rows // max(1, n // 2) // 16) * 16
-    return size, -(-rows // size)
+    plane, _, owning = plane_of(n)
+    owners = plane * owning
+    return -(-rows // owners // 16) * 16, owners
 
 
 def kernel(n, *refs):
     (
         inp, cot, mean, std, w1, b1, g1, s1, w2, b2, g2, s2,
-        bo, eg, GO2, GO1, gvec,
-        XIN, COT, XC, LOW0, LOW1, HS, WF, WD, ACC, WR, PV, ST, VACC, VR,
-        MSG, SLOT, PS2, PS1, GS2, GS1, GR2, GR1, GP2, GP1,
+        bo, eg, GO0, GO1, GO2, gvec,
+        XIN, COT, XC, LOW0, LOW1, HS, WF, WD, ACC, PV, ST, VACC, VR,
+        MSG, SLOT, PS0, PS1, PS2, GS0, GS1, GS2, GR0, GR1, GR2, GP0, GP1, GP2,
         isem, wlsem, wssem, wrsem, msend, mrecv, olsem, ossem, orsem, gsend, grecv, vsem,
     ) = refs
     micro = inp.shape[0]
@@ -43,7 +57,13 @@
     rows = Q * W
     count = float(2 * rows * n)
 
+    plane, all_planes, owning = plane_of(n)
+    first_plane = (all_planes - owning) // 2
+
     me = lax.axis_index("dp")
+    my_plane, my_line = me // plane, me % plane
+    my_piece = my_line * owning + my_plane - first_plane
+    is_owner = (my_plane >= first_plane) & (my_plane < first_plane + owning)
     sec = lax.axis_index("section")
     sib = 1 - sec
 
@@ -69,8 +89,16 @@
     pl.semaphore_signal(barrier, inc=1, device_id={"section": sib}, device_id_type=MESH)
     every_peer(lambda d: pl.semaphore_signal(barrier, inc=1, device_id=peer(d), device_id_type=MESH))
 
+    def raw(b, v):
+        return XC.at[3 * half + 2 * b + v, pl.ds(0, 9)]
+
+    def raw_tap(b, v, k):
+        tap = raw(b, v)[k]
+        return jnp.concatenate([tap[:, :C], tap[:, C:]], axis=0)
+
     for v, ref in enumerate((w1, w2)):
-        pltpu.make_async_copy(ref, WR.at[sec, v], wlsem.at[v]).start()
+        for e in range(2):
+            pltpu.make_async_copy(ref.at[:, e], raw(sec, v).at[:, :, pl.ds(e * C, C)], wlsem.at[v]).start()
     for src, dst, at in ((inp, XIN, 0), (cot, COT, half)):
         for m in range(half):
             for e in range(2):
@@ -92,7 +120,7 @@
         XC[i, Q, :, C : 2 * C] = halo
         return carry
 
-    lax.fori_loop(0, 4 * half, zero_halo, 0)
+    lax.fori_loop(0, 3 * half, zero_halo, 0)
     empty = jnp.zeros((C, C), bf16)
     for i in range(4):
         ACC[i] = jnp.zeros(ACC.shape[1:], f32)
@@ -101,15 +129,15 @@
                 ref[i, j, 0, 0:C, C : 2 * C] = empty
                 ref[i, j, 1, C : 2 * C, 0:C] = empty
     VACC[...] = jnp.zeros(VACC.shape, f32)
-    for ref in (PS2, PS1, GS2, GS1):
+    for ref in (PS0, PS1, PS2, GS0, GS1, GS2):
         ref[...] = jnp.zeros(ref.shape, bf16)
 
     pl.semaphore_wait(barrier, n)
 
     to_sibling(PV.at[sec], PV.at[sec], wssem.at[2], wrsem.at[2])
     for v in range(2):
-        wait(WR.at[sec, v], wlsem.at[v])
-        to_sibling(WR.at[sec, v], WR.at[sec, v], wssem.at[v], wrsem.at[v])
+        wait(raw(sec, v), wlsem.at[v])
+        to_sibling(raw(sec, v), raw(sec, v), wssem.at[v], wrsem.at[v])
 
     def blocks():
         for j in range(3):
@@ -122,11 +150,11 @@
 
     def prep_forward(b, v):
         for i, j, t, r, c in blocks():
-            WF[b * 2 + v, j, t, r, c] = (WR[b, v, i * 3 + j].astype(f32) * 0.5).astype(bf16)
+            WF[b * 2 + v, j, t, r, c] = (raw_tap(b, v, i * 3 + j).astype(f32) * 0.5).astype(bf16)
 
     def prep_backward(b, v):
         for i, j, t, r, c in blocks():
-            WD[b * 2 + v, j, t, r, c] = WR[b, v, (2 - i) * 3 + 2 - j].T
+            WD[b * 2 + v, j, t, r, c] = raw_tap(b, v, (2 - i) * 3 + 2 - j).T
 
     def vec(b, v):
         return PV[b, v : v + 1]
@@ -379,28 +407,32 @@
         send_block([(COT.at[m], eg.at[sec * half + m])], 1, 2)
 
     def back_stage(step, b, stage, own, last, after):
+        def hooks(k, odd):
+            for m, body in after:
+                if m % 2 == odd:
+                    pl.when(k == m // 2)(body)
+
         def pair(k, carry):
             m = 2 * k
             first = lax.div(1, k + 1)
             i = own + (last - own) * first
             x = own * half + m - 1 + ((last - own) * half + half) * first
             step(b, stage, m, low0, (i, XC.at[x], low1))
+            hooks(k, 0)
             step(b, stage, m + 1, low1, (own, xc(own // 2, own % 2, m), low0))
-            for at, body in after:
-                pl.when(k == at)(body)
+            hooks(k, 1)
             return carry
 
         lax.fori_loop(0, half // 2, pair, 0)
 
     def buffers(x):
-        if x == 0:
-            return PS2, GS2, GR2, GP2, GO2
-        return PS1.at[x - 1], GS1.at[x - 1], GR1.at[x - 1], GP1.at[x - 1], GO1.at[x - 1]
+        return ((PS0, PS1, PS2)[x], (GS0, GS1, GS2)[x], (GR0, GR1, GR2)[x], (GP0, GP1, GP2)[x], (GO0, GO1, GO2)[x])
 
     def taps(b, x):
-        a = ACC.at[b * 2 + (1 if x == 0 else 0)]
+        v, columns = PARTS[x]
+        a = ACC.at[b * 2 + v]
         for i in range(3):
-            for j in range(3) if x == 0 else (x - 1,):
+            for at, j in enumerate(columns):
                 out = None
                 for t in range(2):
                     for s in range(2):
@@ -410,7 +442,7 @@
                             c = ((2 - j) * 2 + e) * C
                             d = a[r : r + C, c : c + C]
                             out = d if out is None else out + d
-                yield (i * 3 + j if x == 0 else i) * C, out
+                yield (i * len(columns) + at) * C, out
 
     def to_pair(b, x):
         ps, _, gr, _, _ = buffers(x)
@@ -422,11 +454,9 @@
             to_sibling(ps, gr, gsend.at[x, 0], grecv.at[x, 0])
 
     def piece_size(x):
-        return GP2.shape[1] if x == 0 else GP1.shape[2]
-
-    def owners(x):
-        k = (GO2.shape[0] if x == 0 else GO1.shape[1]) // piece_size(x)
-        return k, (n - k) // 2
+        return buffers(x)[3].shape[1]
+
+    owners = plane * owning
 
     def piece(ref, x, p):
         size = piece_size(x)
@@ -435,68 +465,101 @@
     def span(ref, x, k):
         return ref.at[pl.ds(0, k * piece_size(x))]
 
+    def when_owner(b, mine, other):
+        pl.when((sec == b) & is_owner)(mine)
+        pl.when((sec == b) & jnp.logical_not(is_owner))(other)
+
     def to_owners(b, x):
         _, gs, gr, gp, _ = buffers(x)
-        k, first = owners(x)
 
         @pl.when(sec == b)
         def _():
             wait(gr, grecv.at[x, 0])
             for row, val in taps(b, x):
                 gs[row : row + C] = (val + gr[row : row + C].astype(f32)).astype(bf16)
-            for d in range(k):
-                p = lax.rem(me + d, k)
-
-                @pl.when(first + p == me)
-                def _():
-                    gp[me] = piece(gs, x, p)[...]
-
-                @pl.when(first + p != me)
-                def _():
-                    pltpu.make_async_remote_copy(
-                        piece(gs, x, p), gp.at[me], gsend.at[x, 1], grecv.at[x, 1],
-                        device_id={"dp": first + p}, device_id_type=MESH,
-                    ).start()
-
-    def when_owner(b, x, mine, other):
-        k, first = owners(x)
-        own = (me >= first) & (me < first + k)
-        pl.when((sec == b) & own)(mine)
-        pl.when((sec == b) & jnp.logical_not(own))(other)
-
-    def to_all(b, x):
+
+        def send(p):
+            to = (first_plane + p % owning) * plane + p // owning
+            pltpu.make_async_remote_copy(
+                piece(gs, x, p), gp.at[me], gsend.at[x, 1], grecv.at[x, 1], device_id={"dp": to}, device_id_type=MESH
+            ).start()
+
+        def mine():
+            for d in range(1, owners):
+                send(lax.rem(my_piece + d, owners))
+            gp[me] = piece(gs, x, my_piece)[...]
+
+        def other():
+            for d in range(owners):
+                send(lax.rem(me + d, owners))
+
+        when_owner(b, mine, other)
+
+    def to_all(b, x, direct):
         _, gs, _, gp, go = buffers(x)
-        k, first = owners(x)
 
         def mine():
             if n > 1:
                 wait(gp.at[pl.ds(0, n - 1)], grecv.at[x, 1])
-            if k > 1:
-                wait(span(gs, x, k - 1), gsend.at[x, 1])
+            if owners > 1:
+                wait(span(gs, x, owners - 1), gsend.at[x, 1])
             total = gp[0].astype(f32)
             for d in range(1, n):
                 total = total + gp[d].astype(f32)
-            at = piece(go, x, me - first)
+            at = piece(go, x, my_piece)
             at[...] = total.astype(bf16)
-            every_peer(
-                lambda d: pltpu.make_async_remote_copy(
-                    at, at, gsend.at[x, 2], grecv.at[x, 2], device_id=peer(d), device_id_type=MESH
+
+            def send(to):
+                pltpu.make_async_remote_copy(
+                    at, at, gsend.at[x, 2], grecv.at[x, 2], device_id=to, device_id_type=MESH
                 ).start()
-            )
-
-        when_owner(b, x, mine, lambda: wait(span(gs, x, k), gsend.at[x, 1]))
-
-    def finish(b, x):
-        ps, _, _, gp, go = buffers(x)
-        k, _ = owners(x)
+
+            if direct:
+                every_peer(lambda d: send(peer(d)))
+            else:
+                for d in range(1, all_planes):
+                    send({"dp": lax.rem(my_plane + d, all_planes) * plane + my_line})
+
+        when_owner(b, mine, lambda: wait(span(gs, x, owners), gsend.at[x, 1]))
+
+    def got_pieces(b, x, k):
+        go = buffers(x)[4]
 
         def mine():
             if k > 1:
                 wait(span(go, x, k - 1), grecv.at[x, 2])
-            if n > 1:
-                wait(gp.at[pl.ds(0, n - 1)], gsend.at[x, 2])
-
-        when_owner(b, x, mine, lambda: wait(span(go, x, k), grecv.at[x, 2]))
+
+        when_owner(b, mine, lambda: wait(span(go, x, k), grecv.at[x, 2]))
+
+    def spread(b, x):
+        go = buffers(x)[4]
+        got_pieces(b, x, owning)
+        size = piece_size(x) * owning
+        at = go.at[pl.ds(pl.multiple_of(my_line * size, 16), size)]
+
+        @pl.when(sec == b)
+        def _():
+            for d in range(1, plane):
+                pltpu.make_async_remote_copy(
+                    at, at, gsend.at[x, 3], grecv.at[x, 3],
+                    device_id={"dp": my_plane * plane + lax.rem(my_line + d, plane)}, device_id_type=MESH,
+                ).start()
+
+    def finish(b, x, direct):
+        ps, _, _, gp, go = buffers(x)
+        copies = n - 1 if direct else all_planes - 1
+        if direct:
+            got_pieces(b, x, owners)
+
+        @pl.when(sec == b)
+        def _():
+            if not direct and plane > 1:
+                many = span(go, x, owning * (plane - 1))
+                wait(many, grecv.at[x, 3])
+                wait(many, gsend.at[x, 3])
+
+        if copies > 0:
+            pl.when((sec == b) & is_owner)(lambda: wait(gp.at[pl.ds(0, copies)], gsend.at[x, 2]))
 
         @pl.when(sec != b)
         def _():
@@ -504,7 +567,7 @@
 
     @pl.when(sec != 0)
     def _():
-        wait(WR.at[0, 0], wrsem.at[0])
+        wait(raw(0, 0), wrsem.at[0])
 
     prep_forward(0, 0)
     wait(PV.at[0], wrsem.at[2])
@@ -512,11 +575,11 @@
 
     @pl.when(sec == 0)
     def _():
-        wait(WR.at[0, 0], wrsem.at[0])
-
-    wait(WR.at[0, 1], wrsem.at[1])
+        wait(raw(0, 0), wrsem.at[0])
+
+    wait(raw(0, 1), wrsem.at[1])
     for v in range(2):
-        wait(WR.at[0, 0], wssem.at[v])
+        wait(raw(0, 0), wssem.at[v])
     wait(PV.at[0], wssem.at[2])
     prep_forward(0, 1)
     prep_backward(0, 0)
@@ -526,13 +589,17 @@
     lax.fori_loop(0, half, stage2, 0)
     prep_forward(1, 1)
     prep_backward(1, 1)
+    prep_backward(1, 0)
+    lax.fori_loop(3 * half, 4 * half, zero_halo, 0)
     lax.fori_loop(0, half, stage3, 0)
-    prep_backward(1, 0)
-    w1_parts = (1, 2, 3)
+    w1_parts = (1, 2)
     back_stage(step_e, 1, 4, 3, 3, [])
-    back_stage(
-        step_f, 1, 5, 2, 3, [(0, lambda: to_pair(1, 0)), (half // 2 - 1, lambda: to_owners(1, 0))]
-    )
+    back_stage(step_f, 1, 5, 2, 3, [(0, lambda: to_pair(1, 0)), (1, lambda: to_owners(1, 0))])
+
+    def every_part(phase, b):
+        for x in w1_parts:
+            phase(b, x)
+
     back_stage(
         step_e,
         0,
@@ -540,8 +607,9 @@
         1,
         2,
         [
-            (0, lambda: [to_pair(1, x) for x in w1_parts] and None),
-            (half // 2 - 1, lambda: [to_owners(1, x) for x in w1_parts] and to_all(1, 0)),
+            (0, lambda: every_part(to_pair, 1)),
+            (1, lambda: every_part(to_owners, 1)),
+            (1, lambda: to_all(1, 0, False)),
         ],
     )
     sent_blocks(bo, 0, 0)
@@ -558,22 +626,22 @@
         send_sums(slot(7, m), fold_rows(low_f(last_trio(m), 0, m, coef)))
         if m == 0:
             to_pair(0, 0)
-        if m == 2:
+        if m == 1:
             to_owners(0, 0)
+            spread(1, 0)
+        if m == half - 1:
+            for x in w1_parts:
+                to_all(1, x, False)
     wgrad(0, xc(0, 0, half - 1), last_trio(half - 1), (2, 1))
     to_pair(0, 1)
-    to_pair(0, 2)
 
     def last_column(m, carry):
         wgrad(0, xc(0, 0, m), last_trio(m), (0,))
         return carry
 
     lax.fori_loop(0, half, last_column, 0)
-    to_pair(0, 3)
+    to_pair(0, 2)
     to_owners(0, 1)
-    to_owners(0, 2)
-    for x in w1_parts:
-        to_all(1, x)
     sent_blocks(eg, 1, 2)
 
     def stage8(m, carry):
@@ -585,11 +653,12 @@
 
         @pl.when(m == 0)
         def _():
-            to_owners(0, 3)
-
-        @pl.when(m == 2)
-        def _():
-            to_all(0, 0)
+            to_owners(0, 2)
+
+        @pl.when(m == 1)
+        def _():
+            to_all(0, 0, False)
+            every_part(spread, 1)
 
         return carry
 
@@ -598,8 +667,9 @@
     for m in range(half):
         VACC[0, 0:1] += take_sums(slot(7, m))[0:1]
     to_sibling(VACC.at[sib], VR, vsem.at[0], vsem.at[1])
+    spread(0, 0)
     for x in w1_parts:
-        to_all(0, x)
+        to_all(0, x, True)
     wait(VR, vsem.at[1])
     wait(VR, vsem.at[0])
     gvec[...] = VACC[sec] + VR[...]
@@ -610,13 +680,14 @@
     came_blocks(eg, 1, 2)
     came_blocks(eg, 0, 3)
     for b in (1, 0):
-        for x in range(4):
-            finish(b, x)
+        for x in range(3):
+            finish(b, x, b == 0 and x > 0)
 
 
 def writer(*refs):
-    bo_in, eg_in, go2, go1, gvec, bo, eg, gw1, gw2 = refs[:9]
-    vecs, sem = refs[9:15], refs[15]
+    bo_in, eg_in, *parts = refs[:5]
+    gvec, bo, eg, gw1, gw2 = refs[5:10]
+    vecs, sem = refs[10:16], refs[16]
     copies = []
     for k, (src, dst) in enumerate(((bo_in, bo), (eg_in, eg))):
         for m in range(src.shape[0]):
@@ -625,9 +696,11 @@
                     pltpu.make_async_copy(src.at[m, :, :, pl.ds(e * C, C)], dst.at[m, :, e], sem.at[k, m, e])
                 )
                 copies[-1].start()
-    for k in range(9):
-        gw2[k] = go2[k * C : (k + 1) * C].astype(f32)
-        gw1[k] = go1[k % 3, k // 3 * C : (k // 3 + 1) * C].astype(f32)
+    for ref, (v, columns) in zip(parts, PARTS):
+        for i in range(3):
+            for at, j in enumerate(columns):
+                row = (i * len(columns) + at) * C
+                (gw1, gw2)[v][i * 3 + j] = ref[row : row + C].astype(f32)
     for k, ref in enumerate(vecs):
         ref[...] = gvec[k : k + 1]
     for copy in copies:
@@ -636,8 +709,7 @@
 
 def solution(mesh):
     n = mesh.shape["dp"]
-    size2, own2 = piece_rows(9 * C, n)
-    size1, own1 = piece_rows(3 * C, n)
+    pieces = [piece_rows(part_rows(x), n) for x in range(3)]
 
     def per_device(inputs, channel_mean, channel_std, cotangent, conv_w1, conv_b1, bn_gain1, bn_shift1, conv_w2, conv_b2, bn_gain2, bn_shift2):
         micro, _, H, W, _ = inputs.shape
@@ -649,17 +721,17 @@
         vmem = pl.BlockSpec(memory_space=pltpu.VMEM)
         D = pltpu.SemaphoreType.DMA
         V = pltpu.VMEM
+        whole_parts = [V((size * own, C), bf16) for size, own in pieces]
         mid = pl.pallas_call(
             functools.partial(kernel, n),
             out_shape=[
                 V(pairs, bf16),
                 V(pairs, bf16),
-                V((own2 * size2, C), bf16),
-                V((3, own1 * size1, C), bf16),
+                *whole_parts,
                 V((8, C), f32),
             ],
             in_specs=[anywhere, anywhere, vmem, vmem, anywhere, vmem, vmem, vmem, anywhere, vmem, vmem, vmem],
-            out_specs=[vmem] * 5,
+            out_specs=[vmem] * 6,
             scratch_shapes=[
                 V((half, Q, W, 2 * C), bf16),
                 V((half, Q, W, 2 * C), bf16),
@@ -670,21 +742,16 @@
                 V((4, 3, 2, 2 * C, 2 * C), bf16),
                 V((4, 3, 2, 2 * C, 2 * C), bf16),
                 V((4, 4 * C, 6 * C), f32),
-                V((2, 2, 9, C, C), bf16),
                 V((2, 8, C), f32),
                 V((4, half, 8, C), f32),
                 V((2, 8, C), f32),
                 V((8, C), f32),
                 V((2 * half, 4, C), f32),
                 V((2 * half, n, 4, C), f32),
-                V((own2 * size2, C), bf16),
-                V((3, own1 * size1, C), bf16),
-                V((own2 * size2, C), bf16),
-                V((3, own1 * size1, C), bf16),
-                V((own2 * size2, C), bf16),
-                V((3, own1 * size1, C), bf16),
-                V((n, size2, C), bf16),
-                V((3, n, size1, C), bf16),
+                *whole_parts,
+                *whole_parts,
+                *whole_parts,
+                *[V((n, size, C), bf16) for size, _ in pieces],
                 D((2 * half,)),
                 D((2,)),
                 D((3,)),
@@ -694,8 +761,8 @@
                 D((4,)),
                 D((4,)),
                 D((4,)),
-                D((4, 3)),
-                D((4, 3)),
+                D((3, 4)),
+                D((3, 4)),
                 D((2,)),
             ],
             compiler_params=pltpu.CompilerParams(
@@ -706,11 +773,11 @@
             cotangent.reshape(field),
             channel_mean[None],
             channel_std[None],
-            conv_w1.reshape(9, C, C),
+            conv_w1.reshape(9, 2, C // 2, C),
             conv_b1,
             bn_gain1,
             bn_shift1,
-            conv_w2.reshape(9, C, C),
+            conv_w2.reshape(9, 2, C // 2, C),
             conv_b2,
             bn_gain2,
             bn_shift2,
@@ -724,7 +791,7 @@
                 jax.ShapeDtypeStruct((9, C, C), f32),
             ]
             + [jax.ShapeDtypeStruct((1, C), f32)] * 6,
-            in_specs=[vmem] * 5,
+            in_specs=[vmem] * 6,
             out_specs=[anywhere, anywhere] + [vmem] * 8,
             scratch_shapes=[D((2, micro, 2))],
             compiler_params=pltpu.CompilerParams(vmem_limit_bytes=8 * 2**20),

time: 97.4 us -> 91.1 us (0.935)
  Pallas kernels: 96.4 us -> 90.1 us
    pallas_call x1, Pallas kernels: 91.9 us -> 85.5 us  [per_device(): pl.pallas_call(functools.partial(kernel, n), out_shape=[V(pairs, bf16), V...]
where the time goes in v4:
time: 91.1 us; the launch traced here: 90.9 us
  Pallas kernels  90.1 us (99%)
    pallas_call x1, Pallas kernels, per_device(): pl.pallas_call(functools.partial(kernel, n), out_shape=[V(pairs, bf16), V...  85.5 us
    pallas_call x1, Pallas kernels, per_device(): pl.pallas_call(writer, out_shape=[jax.ShapeDtypeStruct(field, bf16), jax....  4.57 us

profile of v4, /device:TPU:0, one launch (start us, length us, event | category | flops | bytes accessed | tf_op | source)
XLA Modules:
  0.0 90.9 jit_solution(11202240213952021177)
XLA Ops:
  0.6 85.5 %shard_map.195 = (bf16[8,16,64,256]{3,2,1,0:T(8,128)(2,1)S(1)}, bf16[8,16,64,256]{3,2,1,0:T(8,128)(2,1)S(1)}, bf16[1152,128]{1,0:T(8,128)(2,1)S(1)}, bf16[768,12...) custom-call(bf16[8,16,2,64,128]{4,3,2,1,0:T(8,128)(2,1)} %bitcast.14, ...), custom_call_target="tpu_custom_call" | custom-call | tf_op jit(solution)/shard_map/pallas_call | solution.py:725
  86.2 4.6 %shard_map.196 = (bf16[8,16,2,64,128]{4,3,2,1,0:T(8,128)(2,1)}, bf16[8,16,2,64,128]{4,3,2,1,0:T(8,128)(2,1)}, f32[9,128,128]{2,1,0:T(8,128)}, f32[9,128,128]{2,1...) custom-call(bf16[8,16,64,256]{3,2,1,0:T(8,128)(2,1)S(1)} %get-tuple-, ...), custom_call_target="tpu_custom_call" | custom-call | tf_op jit(solution)/shard_map/pallas_call | solution.py:785

commit v5 on v4

--- a/solution.py
+++ b/solution.py
@@ -47,7 +47,7 @@
         inp, cot, mean, std, w1, b1, g1, s1, w2, b2, g2, s2,
         bo, eg, GO0, GO1, GO2, gvec,
         XIN, COT, XC, LOW0, LOW1, HS, WF, WD, ACC, PV, ST, VACC, VR,
-        MSG, SLOT, PS0, PS1, PS2, GS0, GS1, GS2, GR0, GR1, GR2, GP0, GP1, GP2,
+        MSG, SLOT, PS0, PS1, PS2, GR0, GR1, GR2, GP0, GP1, GP2,
         isem, wlsem, wssem, wrsem, msend, mrecv, olsem, ossem, orsem, gsend, grecv, vsem,
     ) = refs
     micro = inp.shape[0]
@@ -129,7 +129,7 @@
                 ref[i, j, 0, 0:C, C : 2 * C] = empty
                 ref[i, j, 1, C : 2 * C, 0:C] = empty
     VACC[...] = jnp.zeros(VACC.shape, f32)
-    for ref in (PS0, PS1, PS2, GS0, GS1, GS2):
+    for ref in (PS0, PS1, PS2):
         ref[...] = jnp.zeros(ref.shape, bf16)
 
     pl.semaphore_wait(barrier, n)
@@ -426,7 +426,7 @@
         lax.fori_loop(0, half // 2, pair, 0)
 
     def buffers(x):
-        return ((PS0, PS1, PS2)[x], (GS0, GS1, GS2)[x], (GR0, GR1, GR2)[x], (GP0, GP1, GP2)[x], (GO0, GO1, GO2)[x])
+        return ((PS0, PS1, PS2)[x], (GR0, GR1, GR2)[x], (GR0, GR1, GR2)[x], (GP0, GP1, GP2)[x], (GO0, GO1, GO2)[x])
 
     def taps(b, x):
         v, columns = PARTS[x]
@@ -593,7 +593,7 @@
     lax.fori_loop(3 * half, 4 * half, zero_halo, 0)
     lax.fori_loop(0, half, stage3, 0)
     w1_parts = (1, 2)
-    back_stage(step_e, 1, 4, 3, 3, [])
+    back_stage(step_e, 1, 4, 3, 2, [])
     back_stage(step_f, 1, 5, 2, 3, [(0, lambda: to_pair(1, 0)), (1, lambda: to_owners(1, 0))])
 
     def every_part(phase, b):
@@ -748,7 +748,6 @@
                 V((8, C), f32),
                 V((2 * half, 4, C), f32),
                 V((2 * half, n, 4, C), f32),
-                *whole_parts,
                 *whole_parts,
                 *whole_parts,
                 *[V((n, size, C), bf16) for size, _ in pieces],

time: 91.1 us -> 89.6 us (0.984)
  Pallas kernels: 90.1 us -> 88.6 us
    pallas_call x1, Pallas kernels: 85.5 us -> 84 us  [per_device(): pl.pallas_call(functools.partial(kernel, n), out_shape=[V(pairs, bf16), V...]
where the time goes in v5:
time: 89.6 us; the launch traced here: 89.4 us
  Pallas kernels  88.6 us (99%)
    pallas_call x1, Pallas kernels, per_device(): pl.pallas_call(functools.partial(kernel, n), out_shape=[V(pairs, bf16), V...  84 us
    pallas_call x1, Pallas kernels, per_device(): pl.pallas_call(writer, out_shape=[jax.ShapeDtypeStruct(field, bf16), jax....  4.57 us

profile of v5, /device:TPU:0, one launch (start us, length us, event | category | flops | bytes accessed | tf_op | source)
XLA Modules:
  0.0 89.4 jit_solution(17234748022134493040)
XLA Ops:
  0.6 84.0 %shard_map.195 = (bf16[8,16,64,256]{3,2,1,0:T(8,128)(2,1)S(1)}, bf16[8,16,64,256]{3,2,1,0:T(8,128)(2,1)S(1)}, bf16[1152,128]{1,0:T(8,128)(2,1)S(1)}, bf16[768,12...) custom-call(bf16[8,16,2,64,128]{4,3,2,1,0:T(8,128)(2,1)} %bitcast.14, ...), custom_call_target="tpu_custom_call" | custom-call | tf_op jit(solution)/shard_map/pallas_call | solution.py:725
  84.7 4.6 %shard_map.196 = (bf16[8,16,2,64,128]{4,3,2,1,0:T(8,128)(2,1)}, bf16[8,16,2,64,128]{4,3,2,1,0:T(8,128)(2,1)}, f32[9,128,128]{2,1,0:T(8,128)}, f32[9,128,128]{2,1...) custom-call(bf16[8,16,64,256]{3,2,1,0:T(8,128)(2,1)S(1)} %get-tuple-, ...), custom_call_target="tpu_custom_call" | custom-call | tf_op jit(solution)/shard_map/pallas_call | solution.py:784

commit v6 on v5

--- a/solution.py
+++ b/solution.py
@@ -655,7 +655,7 @@
         def _():
             to_owners(0, 2)
 
-        @pl.when(m == 1)
+        @pl.when(m == 0)
         def _():
             to_all(0, 0, False)
             every_part(spread, 1)

time: 89.6 us -> 89.3 us (level)
  no operation moved by 1% of the time
where the time goes in v6:
time: 89.3 us; the launch traced here: 89.2 us
  Pallas kernels  88.3 us (99%)
    pallas_call x1, Pallas kernels, per_device(): pl.pallas_call(functools.partial(kernel, n), out_shape=[V(pairs, bf16), V...  83.8 us
    pallas_call x1, Pallas kernels, per_device(): pl.pallas_call(writer, out_shape=[jax.ShapeDtypeStruct(field, bf16), jax....  4.57 us

profile of v6, /device:TPU:0, one launch (start us, length us, event | category | flops | bytes accessed | tf_op | source)
XLA Modules:
  0.0 89.2 jit_solution(3727474650235740321)
XLA Ops:
  0.6 83.8 %shard_map.195 = (bf16[8,16,64,256]{3,2,1,0:T(8,128)(2,1)S(1)}, bf16[8,16,64,256]{3,2,1,0:T(8,128)(2,1)S(1)}, bf16[1152,128]{1,0:T(8,128)(2,1)S(1)}, bf16[768,12...) custom-call(bf16[8,16,2,64,128]{4,3,2,1,0:T(8,128)(2,1)} %bitcast.14, ...), custom_call_target="tpu_custom_call" | custom-call | tf_op jit(solution)/shard_map/pallas_call | solution.py:725
  84.4 4.6 %shard_map.196 = (bf16[8,16,2,64,128]{4,3,2,1,0:T(8,128)(2,1)}, bf16[8,16,2,64,128]{4,3,2,1,0:T(8,128)(2,1)}, f32[9,128,128]{2,1,0:T(8,128)}, f32[9,128,128]{2,1...) custom-call(bf16[8,16,64,256]{3,2,1,0:T(8,128)(2,1)S(1)} %get-tuple-, ...), custom_call_target="tpu_custom_call" | custom-call | tf_op jit(solution)/shard_map/pallas_call | solution.py:784
